TPU v7x, 32 devices: a whole 2x2x4 slice. The times are simulated.
32 devices in a mesh: narrow: 4 (over x, core), wide: 8 (over z, y).
Axes of the slice: x: 2, y: 2, z: 4, core: 2. Of those that a mesh axis runs over, the one named last changes fastest.
Arguments:
- tokens: bfloat16 [8, 1024, 1024], P('wide', 'narrow'), may hold values from -6 to 6
- segments: int32 [8, 1024], P('wide'), may hold values from 0 to 8, as said below
- routes: int32 [8192, 1], P(('narrow', 'wide')), may hold values from 0 to 7; in each aligned block of 256 rows (0 to 255, 256 to 511, ...) at most 64 rows name the same one
- w_qkv: bfloat16 [1024, 3072], replicated, may hold values from -0.1875 to 0.1875
- w_out: bfloat16 [1024, 1024], replicated, may hold values from -1 to 1
- w_fc1: bfloat16 [1024, 4096], replicated, may hold values from -0.1875 to 0.1875
- w_fc2: bfloat16 [4096, 1024], replicated, may hold values from -0.1875 to 0.1875
- router: bfloat16 [1024, 8], replicated, may hold values from -0.09375 to 0.09375
- mix_weight: bfloat16 [1024, 2], replicated, may hold values from -0.1875 to 0.1875
- gain_one: bfloat16 [1024], replicated, may hold values from 0.5 to 1.5
- gain_two: bfloat16 [1024], replicated, may hold values from 0.5 to 1.5
- expert_in: bfloat16 [8, 1024, 4096], P('wide'), may hold values from -0.1875 to 0.1875
- expert_out: bfloat16 [8, 4096, 1024], P('wide'), may hold values from -1 to 1
- cotangent: bfloat16 [8, 1024, 1024], P('wide', 'narrow'), may hold values from -6 to 6
Outputs:
- output: bfloat16 [8, 1024, 1024], P('wide', 'narrow')
- input_grad: float32 [8, 1024, 1024], P('wide', 'narrow')
- grad_qkv: float32 [1024, 3072], P('wide')
- grad_out: float32 [1024, 1024], P('wide')
- grad_fc1: float32 [1024, 4096], P('wide')
- grad_fc2: float32 [4096, 1024], P('wide')
- grad_router: float32 [1024, 8], P('wide')
- grad_mix: float32 [1024, 2], P('wide')
- grad_gain_one: float32 [1024], P('wide')
- grad_gain_two: float32 [1024], P('wide')
- grad_expert_in: float32 [8, 1024, 4096], P('wide', 'narrow')
- grad_expert_out: float32 [8, 4096, 1024], P('wide', 'narrow')
Inputs may be any that keep to these rules, and one draw needn't show every extreme that they name: `routes`: in each aligned block of 256 rows (the rows of one device) no expert is named more than 64 times. `segments`: never decreases along a sequence and starts at 0.
All inputs are finite; a program needn't handle non-finite values.
Results may differ from a plain program's by a relative error of at most 0.015.
Values may be sent and summed in bfloat16 or wider, within the bound.
No kernel may reach another device: no remote copies, remote signals or barrier semaphores. Data moves between devices by JAX's collectives and lax.ppermute only.
A program may use at most 256 MiB of HBM per device.

v0:
```python
import jax
import jax.numpy as jnp
from jax import lax
from jax.sharding import PartitionSpec as P

HEADS = 16
HEAD_DIM = 64


EPSILON = 1e-05
NEGATIVE_FILL = -1e30


def normalize(values, gain):
    centred = values - jnp.mean(values, axis=-1, keepdims=True)
    spread = lax.rsqrt(jnp.mean(centred * centred, axis=-1, keepdims=True) + EPSILON)
    scaled = centred * spread
    return (scaled * gain, scaled, spread)


def normal_back(incoming, scaled, spread, gain):
    inner = incoming * gain
    result = spread * (
        inner
        - jnp.mean(inner, axis=-1, keepdims=True)
        - scaled * jnp.mean(inner * scaled, axis=-1, keepdims=True)
    )
    return (result, jnp.sum(incoming * scaled, axis=0))


def smooth(values):
    return jax.nn.gelu(values, approximate=True)


def smooth_back(values, incoming):
    pullback = jax.vjp(smooth, values)[1]
    return pullback(incoming)[0]


def across(left, right):
    return lax.dot_general(
        left, right, (((0,), (0,)), ((), ())), preferred_element_type=jnp.float32
    )


def beside(left, right):
    return lax.dot_general(
        left, right, (((1,), (1,)), ((), ())), preferred_element_type=jnp.float32
    )


def masked_scores(query_three, keys_three, segment_row, first_pos, scale):
    local_len = query_three.shape[0]
    full_len = keys_three.shape[0]
    scores = (
        jnp.einsum("qhd,khd->hqk", query_three, keys_three, preferred_element_type=jnp.float32)
        * scale
    )
    query_pos = first_pos + jnp.arange(local_len)
    key_pos = jnp.arange(full_len)
    query_seg = lax.dynamic_slice_in_dim(segment_row, first_pos, local_len, 0)
    allowed = (key_pos[None, :] <= query_pos[:, None]) & (
        segment_row[None, :] == query_seg[:, None]
    )
    return jnp.where(allowed[None], scores, NEGATIVE_FILL)


def per_device(
    tokens,
    segments,
    routes,
    w_qkv,
    w_out,
    w_fc1,
    w_fc2,
    router,
    mix_weight,
    gain_one,
    gain_two,
    expert_in,
    expert_out,
    cotangent,
):
    seq_count, local_len, model_width = tokens.shape
    tok_rows = seq_count * local_len
    full_len = segments.shape[1]
    experts_all = router.shape[1]
    capacity = 2 * tok_rows // experts_all
    wide_count = lax.axis_size("wide")
    local_experts = expert_in.shape[0]
    scale = HEAD_DIM ** (-0.5)
    first_pos = lax.axis_index("narrow") * local_len
    gain_first = gain_one.astype(jnp.float32)
    gain_second = gain_two.astype(jnp.float32)
    inputs = tokens.reshape(tok_rows, model_width).astype(jnp.float32)
    normed_one, scaled_one, spread_one = normalize(inputs, gain_first)
    first = normed_one.astype(jnp.bfloat16)
    projected = jnp.dot(first, w_qkv, preferred_element_type=jnp.float32)
    queries = projected[:, :model_width].astype(jnp.bfloat16)
    local_kv = (
        projected[:, model_width:]
        .astype(jnp.bfloat16)
        .reshape(seq_count, local_len, 2 * model_width)
    )
    whole_kv = lax.all_gather(local_kv, "narrow", axis=1, tiled=True)
    query_four = queries.reshape(seq_count, local_len, HEADS, HEAD_DIM)

    def attend_one(members):
        query_three, kv_rows, segment_row = members
        keys_three = kv_rows[:, :model_width].reshape(full_len, HEADS, HEAD_DIM)
        values_three = kv_rows[:, model_width:].reshape(full_len, HEADS, HEAD_DIM)
        masked = masked_scores(query_three, keys_three, segment_row, first_pos, scale)
        highest = jnp.max(masked, axis=-1, keepdims=True)
        weights = jnp.exp(masked - highest)
        totals = jnp.sum(weights, axis=-1, keepdims=True)
        probs = (weights / totals).astype(jnp.bfloat16)
        mixed_rows = jnp.einsum(
            "hqk,khd->qhd", probs, values_three, preferred_element_type=jnp.float32
        )
        return (
            mixed_rows.reshape(local_len, model_width).astype(jnp.bfloat16),
            highest + jnp.log(totals),
        )

    attended, log_total = lax.map(attend_one, (query_four, whole_kv, segments))
    attended = attended.reshape(tok_rows, model_width)
    mid = inputs + jnp.dot(attended, w_out, preferred_element_type=jnp.float32)
    normed_two, scaled_two, spread_two = normalize(mid, gain_second)
    second = normed_two.astype(jnp.bfloat16)
    dense_pre = jnp.dot(second, w_fc1, preferred_element_type=jnp.float32)
    dense_hidden = smooth(dense_pre).astype(jnp.bfloat16)
    dense_result = jnp.dot(dense_hidden, w_fc2, preferred_element_type=jnp.float32)
    route_probs = jax.nn.softmax(
        jnp.dot(second, router, preferred_element_type=jnp.float32), axis=-1
    )
    chosen = routes == jnp.arange(experts_all)[None, :]
    onehot = chosen.astype(jnp.float32)
    gate = jnp.sum(route_probs * onehot, axis=-1, keepdims=True)
    mixing = jax.nn.softmax(
        jnp.dot(second, mix_weight, preferred_element_type=jnp.float32), axis=-1
    )
    chosen_int = chosen.astype(jnp.int32)
    earlier = jnp.cumsum(chosen_int, axis=0) - 1
    position = jnp.sum(earlier * chosen_int, axis=1)
    slot_index = routes[:, 0] * capacity + position
    outbound = (
        jnp.zeros((experts_all * capacity, model_width), jnp.bfloat16).at[slot_index].set(second)
    )
    outbound = outbound.reshape(experts_all, capacity, model_width)
    received = lax.all_to_all(outbound, "wide", split_axis=0, concat_axis=0, tiled=True)
    grouped_in = received.reshape(wide_count, local_experts, received.shape[1], model_width)
    expert_pre = jnp.einsum(
        "wend,edf->wenf", grouped_in, expert_in, preferred_element_type=jnp.float32
    )
    expert_hidden = smooth(expert_pre).astype(jnp.bfloat16)
    produced = jnp.einsum(
        "wenf,efd->wend", expert_hidden, expert_out, preferred_element_type=jnp.float32
    )
    produced = produced.astype(jnp.bfloat16).reshape(received.shape)
    returned_rows = lax.all_to_all(produced, "wide", split_axis=0, concat_axis=0, tiled=True)
    expert_result = returned_rows.reshape(experts_all * capacity, model_width)[slot_index].astype(
        jnp.float32
    )
    result = mid + mixing[:, 0:1] * dense_result + mixing[:, 1:2] * gate * expert_result
    output = result.astype(jnp.bfloat16).reshape(seq_count, local_len, model_width)
    d_output = cotangent.reshape(tok_rows, model_width).astype(jnp.float32)
    mix_terms = jnp.concatenate(
        [
            jnp.sum(d_output * dense_result, axis=-1, keepdims=True),
            jnp.sum(d_output * gate * expert_result, axis=-1, keepdims=True),
        ],
        axis=1,
    )
    d_mix_logits = (
        mixing * (mix_terms - jnp.sum(mixing * mix_terms, axis=-1, keepdims=True))
    ).astype(jnp.bfloat16)
    d_gate = jnp.sum(d_output * mixing[:, 1:2] * expert_result, axis=-1, keepdims=True)
    d_route_logits = (route_probs * (onehot - gate) * d_gate).astype(jnp.bfloat16)
    d_dense = (d_output * mixing[:, 0:1]).astype(jnp.bfloat16)
    grad_fc2 = across(dense_hidden, d_dense)
    d_dense_pre = smooth_back(dense_pre, beside(d_dense, w_fc2)).astype(jnp.bfloat16)
    grad_fc1 = across(second, d_dense_pre)
    grad_router = across(second, d_route_logits)
    grad_mix = across(second, d_mix_logits)
    d_expert = (d_output * mixing[:, 1:2] * gate).astype(jnp.bfloat16)
    outgoing = (
        jnp.zeros((experts_all * capacity, model_width), jnp.bfloat16).at[slot_index].set(d_expert)
    )
    outgoing = outgoing.reshape(experts_all, capacity, model_width)
    arriving = lax.all_to_all(outgoing, "wide", split_axis=0, concat_axis=0, tiled=True)
    grouped_in = received.reshape(wide_count, local_experts, capacity, model_width)
    grouped_grad = arriving.reshape(wide_count, local_experts, capacity, model_width)
    expert_pre = jnp.einsum(
        "wend,edf->wenf", grouped_in, expert_in, preferred_element_type=jnp.float32
    )
    expert_hidden = smooth(expert_pre).astype(jnp.bfloat16)
    grad_expert_out = jnp.einsum(
        "wenf,wend->efd", expert_hidden, grouped_grad, preferred_element_type=jnp.float32
    )
    hidden_grad = jnp.einsum(
        "wend,efd->wenf", grouped_grad, expert_out, preferred_element_type=jnp.float32
    )
    d_expert_pre = smooth_back(expert_pre, hidden_grad).astype(jnp.bfloat16)
    grad_expert_in = jnp.einsum(
        "wend,wenf->edf", grouped_in, d_expert_pre, preferred_element_type=jnp.float32
    )
    d_sent = jnp.einsum(
        "wenf,edf->wend", d_expert_pre, expert_in, preferred_element_type=jnp.float32
    )
    d_sent = d_sent.astype(jnp.bfloat16).reshape(received.shape)
    d_return = lax.all_to_all(d_sent, "wide", split_axis=0, concat_axis=0, tiled=True)
    d_back = d_return.reshape(experts_all * capacity, model_width)[slot_index].astype(jnp.float32)
    grad_expert_in, grad_expert_out = (
        lax.psum_scatter(
            grad_expert_in.astype(jnp.bfloat16), "narrow", scatter_dimension=1, tiled=True
        ).astype(jnp.float32),
        lax.psum_scatter(
            grad_expert_out.astype(jnp.bfloat16), "narrow", scatter_dimension=1, tiled=True
        ).astype(jnp.float32),
    )
    d_second = (
        beside(d_dense_pre, w_fc1)
        + d_back
        + beside(d_route_logits, router)
        + beside(d_mix_logits, mix_weight)
    )
    d_normed_two, grad_gain_two = normal_back(d_second, scaled_two, spread_two, gain_second)
    d_mid = d_output + d_normed_two
    d_attn = d_mid.astype(jnp.bfloat16)
    grad_out = across(attended, d_attn)
    d_attended = (
        beside(d_attn, w_out).astype(jnp.bfloat16).reshape(seq_count, local_len, HEADS, HEAD_DIM)
    )

    def attend_back(members):
        query_three, kv_rows, segment_row, log_rows, d_rows = members
        keys_three = kv_rows[:, :model_width].reshape(full_len, HEADS, HEAD_DIM)
        values_three = kv_rows[:, model_width:].reshape(full_len, HEADS, HEAD_DIM)
        masked_back = masked_scores(query_three, keys_three, segment_row, first_pos, scale)
        softened = jnp.exp(masked_back - log_rows)
        softened_low = softened.astype(jnp.bfloat16)
        d_values = jnp.einsum(
            "hqk,qhd->khd", softened_low, d_rows, preferred_element_type=jnp.float32
        )
        d_probs = jnp.einsum(
            "qhd,khd->hqk", d_rows, values_three, preferred_element_type=jnp.float32
        )
        d_scores = (
            softened * (d_probs - jnp.sum(d_probs * softened, axis=-1, keepdims=True))
        ).astype(jnp.bfloat16)
        d_queries = (
            jnp.einsum("hqk,khd->qhd", d_scores, keys_three, preferred_element_type=jnp.float32)
            * scale
        )
        d_keys = (
            jnp.einsum("hqk,qhd->khd", d_scores, query_three, preferred_element_type=jnp.float32)
            * scale
        )
        d_kv_rows = jnp.concatenate(
            [d_keys.reshape(full_len, model_width), d_values.reshape(full_len, model_width)],
            axis=-1,
        )
        return (d_queries.astype(jnp.bfloat16).reshape(local_len, model_width), d_kv_rows)

    d_queries, d_kv = lax.map(attend_back, (query_four, whole_kv, segments, log_total, d_attended))
    d_queries = d_queries.reshape(tok_rows, model_width)
    d_kv_local = lax.psum_scatter(
        d_kv.astype(jnp.bfloat16), "narrow", scatter_dimension=1, tiled=True
    ).reshape(tok_rows, 2 * model_width)
    d_projected = jnp.concatenate([d_queries, d_kv_local], axis=1)
    grad_qkv = across(first, d_projected)
    d_first = beside(d_projected, w_qkv)
    d_inputs, grad_gain_one = normal_back(d_first, scaled_one, spread_one, gain_first)
    input_grad = (d_mid + d_inputs).reshape(seq_count, local_len, model_width)
    summed = (
        lax.psum_scatter(grad_qkv, "wide", scatter_dimension=0, tiled=True),
        lax.psum_scatter(grad_out, "wide", scatter_dimension=0, tiled=True),
        lax.psum_scatter(grad_fc1, "wide", scatter_dimension=0, tiled=True),
        lax.psum_scatter(grad_fc2, "wide", scatter_dimension=0, tiled=True),
        lax.psum_scatter(grad_router, "wide", scatter_dimension=0, tiled=True),
        lax.psum_scatter(grad_mix, "wide", scatter_dimension=0, tiled=True),
        lax.psum_scatter(grad_gain_one, "wide", scatter_dimension=0, tiled=True),
        lax.psum_scatter(grad_gain_two, "wide", scatter_dimension=0, tiled=True),
    )
    part_qkv, part_out, part_fc1, part_fc2, part_router, part_mix, part_first, part_second = summed
    grad_qkv, grad_out, grad_fc1, grad_fc2, grad_router, grad_mix, grad_gain_one, grad_gain_two = (
        lax.psum(part_qkv.astype(jnp.bfloat16), "narrow").astype(jnp.float32),
        lax.psum(part_out.astype(jnp.bfloat16), "narrow").astype(jnp.float32),
        lax.psum(part_fc1.astype(jnp.bfloat16), "narrow").astype(jnp.float32),
        lax.psum(part_fc2.astype(jnp.bfloat16), "narrow").astype(jnp.float32),
        lax.psum(part_router.astype(jnp.bfloat16), "narrow").astype(jnp.float32),
        lax.psum(part_mix.astype(jnp.bfloat16), "narrow").astype(jnp.float32),
        lax.psum(part_first.astype(jnp.bfloat16), "narrow").astype(jnp.float32),
        lax.psum(part_second.astype(jnp.bfloat16), "narrow").astype(jnp.float32),
    )
    return (
        output,
        input_grad,
        grad_qkv,
        grad_out,
        grad_fc1,
        grad_fc2,
        grad_router,
        grad_mix,
        grad_gain_one,
        grad_gain_two,
        grad_expert_in,
        grad_expert_out,
    )


def solution(mesh):
    return jax.shard_map(
        per_device,
        mesh=mesh,
        in_specs=(
            P("wide", "narrow", None),
            P("wide", None),
            P(("narrow", "wide"), None),
            P(),
            P(),
            P(),
            P(),
            P(),
            P(),
            P(),
            P(),
            P("wide", None, None),
            P("wide", None, None),
            P("wide", "narrow", None),
        ),
        out_specs=(
            P("wide", "narrow", None),
            P("wide", "narrow", None),
            P("wide", None),
            P("wide", None),
            P("wide", None),
            P("wide", None),
            P("wide", None),
            P("wide", None),
            P("wide"),
            P("wide"),
            P("wide", "narrow", None),
            P("wide", "narrow", None),
        ),
        check_vma=False,
    )
```

profile of v0, /device:TPU:0, one launch (start us, length us, event | category | flops | bytes accessed | tf_op | source)
XLA Modules:
  0.0 1545.4 jit_solution(12493230938406525774)
XLA Ops:
  20.4 34.7 %all-gather.3.cloned.1.call-done = bf16[1024,2048]{1,0:T(8,128)(2,1)} async-done(((bf16[256,2048]{1,0:T(8,128)(2,1)}), bf16[1024,2048]{1,0:T(8,128)(2,1)}) %all-gather.3.cloned.1.call-update) | async-done | bytes 4194320 | tf_op jit(solution)/shard_map/all_gather | solution.py:105
  97.3 21.5 %all-to-all-done = bf16[8,64,1024]{2,1,0:T(8,128)(2,1)} async-done(((bf16[8,64,1024]{2,1,0:T(8,128)(2,1)}), bf16[8,64,1024]{2,1,0:T(8,128)(2,1)}, u32[]{:S(2)}, u32[]{:S(2)}) %all-to-all-start) | async-done | bytes 1048608 | tf_op jit(solution)/shard_map/all_to_all | solution.py:150
  123.1 7.2 fusion.21
  133.6 9.6 fusion.47
  153.0 12.7 fusion.29
  167.6 8.0 fusion.44
  182.6 8.8 reduce-scatter.12.cloned.1.call-start
  197.4 10.8 fusion.38
  215.7 8.6 fusion.76
  224.4 6.0 convolution_add_fusion.3
  233.9 7.9 fusion.41
  241.8 11.0 multiply_reduce_fusion
  252.8 11.8 multiply_convert_fusion
  273.6 11.4 fusion.94
  286.0 9.7 fusion.128
  295.8 6.8 fusion.53
  302.7 12.4 reduce-scatter.12.cloned.1.call-done
  315.1 7.8 fusion.80
  325.2 13.2 fusion.26
  338.5 10.4 fusion.25
  349.2 57.9 %reduce-scatter.16.cloned.1.call-done = f32[128,1024]{1,0:T(8,128)} async-done(((f32[1024,1024]{1,0:T(8,128)}), f32[128,1024]{1,0:T(8,128)}) %reduce-scatter.16.cloned.1.call-update) | async-done | bytes 524304 | tf_op jit(solution)/shard_map/reduce_scatter | solution.py:277
  408.9 283.6 %reduce-scatter.20.cloned.1.call-done = f32[512,1024]{1,0:T(8,128)} async-done(((f32[4096,1024]{1,0:T(8,128)}), f32[512,1024]{1,0:T(8,128)}) %reduce-scatter.20.cloned.1.call-update) | async-done | bytes 2097168 | tf_op jit(solution)/shard_map/reduce_scatter | solution.py:279
  695.2 283.1 %reduce-scatter.18.cloned.1.call-done = f32[128,4096]{1,0:T(8,128)} async-done(((f32[1024,4096]{1,0:T(8,128)}), f32[128,4096]{1,0:T(8,128)}) %reduce-scatter.18.cloned.1.call-update) | async-done | bytes 2097168 | tf_op jit(solution)/shard_map/reduce_scatter | solution.py:278
  981.0 207.2 %reduce-scatter.14.cloned.1.call-done = f32[128,3072]{1,0:T(8,128)} async-done(((f32[1024,3072]{1,0:T(8,128)}), f32[128,3072]{1,0:T(8,128)}) %reduce-scatter.14.cloned.1.call-update) | async-done | bytes 1572880 | tf_op jit(solution)/shard_map/reduce_scatter | solution.py:276
  1191.9 61.3 %reduce-scatter.28.cloned.1.call-done = f32[128,2]{1,0:T(8,128)} async-done(((f32[1024,2]{1,0:T(8,128)}), f32[128,2]{1,0:T(8,128)}) %reduce-scatter.28.cloned.1.call-update) | async-done | bytes 1040
  1254.2 55.7 %reduce-scatter.22.cloned.1.call-done = f32[128,8]{0,1:T(8,128)} async-done(((f32[1024,8]{0,1:T(8,128)}), f32[128,8]{0,1:T(8,128)}) %reduce-scatter.22.cloned.1.call-update) | async-done | bytes 4112 | tf_op jit(solution)/shard_map/reduce_scatter | solution.py:280
  1310.5 6.1 fusion.71
  1316.6 19.7 %all-reduce.2 = (bf16[1024]{0:T(1024)(128)(2,1)S(1)}, bf16[1024]{0:T(1024)(128)(2,1)S(1)}) all-reduce(f32[1024]{0:T(1024)S(1)} %get-tuple-element.53, f32[1024]{0:T(1024)S(1)} %get-tuple-element.51), channel_id=10, replica_groups=mesh['narrow'=4,'wide'=8] {'wide'}, use_global_device_ids=true, to_apply=%region_39.40.clone | all-reduce | flops 2048 | bytes 12288
  1336.4 6.2 all-reduce.3
  1347.3 36.1 %reduce-scatter.26.cloned.1.call-done = bf16[1,1024,1024]{2,1,0:T(8,128)(2,1)} async-done(((bf16[1,4096,1024]{2,1,0:T(8,128)(2,1)}), bf16[1,1024,1024]{2,1,0:T(8,128)(2,1)}) %reduce-scatter.26.cloned.1.call-update) | async-done | bytes 2097168 | tf_op jit(solution)/shard_map/reduce_scatter | solution.py:217
  1387.5 70.0 %reduce-scatter.24.cloned.1.call-done = bf16[1,256,4096]{2,1,0:T(8,128)(2,1)} async-done(((bf16[1,1024,4096]{2,1,0:T(8,128)(2,1)}), bf16[1,256,4096]{2,1,0:T(8,128)(2,1)}) %reduce-scatter.24.cloned.1.call-update) | async-done | bytes 2097168 | tf_op jit(solution)/shard_map/reduce_scatter | solution.py:214
  1461.8 68.2 %all-reduce.7.cloned.1.call-done = (bf16[128,3072]{1,0:T(8,128)(2,1)}, bf16[128,1024]{1,0:T(8,128)(2,1)}, bf16[128,4096]{1,0:T(8,128)(2,1)}, bf16[512,1024]{1,0:T(8,128)(2,1)}) async-done(((bf16[128,3072]{1,0:T(8,128)(2,1)}, bf16[128,1024]{1,0:T(8,128)(2,1)}, bf16[128,4096]{1,0:T(8,128)(2,1)}, bf16[512,1024]{1,0:T(8,128)(2,1)}), (bf16[128,3072]{1,0:T(8,128)(2,1)}, bf16[128,1024]{1,0:T(8,128)(2,1)}, ...) | async-done | bytes 3145744 | tf_op jit(solution)/shard_map/psum | solution.py:287
  (183 shorter events, 144.4 us)
Async XLA Ops:
  7.2 75.7 %copy-start = (bf16[1024,1024]{1,0:T(8,128)(2,1)S(1)}, bf16[1024,1024]{1,0:T(8,128)(2,1)}, u32[]{:S(2)}) copy-start(bf16[1024,1024]{1,0:T(8,128)(2,1)} %param.18) | copy-start | bytes 6291460
  7.2 47.9 %all-gather.3.cloned.1.call-start = ((), (), s32[]{:S(2)}) async-start(), calls=%async_computation.21 | async-start | bytes 5242880 | tf_op jit(solution)/shard_map/all_gather | solution.py:105
  10.6 8.3 copy-start.34
  10.6 8.3 copy-start.27
  10.6 9.4 copy-start.33
  20.0 47.7 %copy-start.12 = (bf16[256,1024]{0,1:T(8,128)(2,1)}, bf16[256,1024]{0,1:T(8,128)(2,1)S(1)}, u32[]{:S(2)}) copy-start(bf16[256,1024]{0,1:T(8,128)(2,1)S(1)} %copy.39) | copy-start | bytes 1572868
  82.9 10.0 copy-start.30
  82.9 10.8 copy-start.26
  86.8 32.0 %all-to-all-start = ((bf16[8,64,1024]{2,1,0:T(8,128)(2,1)}), bf16[8,64,1024]{2,1,0:T(8,128)(2,1)}, u32[]{:S(2)}, u32[]{:S(2)}) async-start(bf16[8,64,1024]{2,1,0:T(8,128)(2,1)} %bitcast.231), calls=%async_computation | async-start | bytes 2097152 | tf_op jit(solution)/shard_map/all_to_all | solution.py:150
  118.8 29.9 %all-to-all-start.2 = ((bf16[8,64,1024]{2,1,0:T(8,128)(2,1)}), bf16[8,64,1024]{2,1,0:T(8,128)(2,1)}, u32[]{:S(2)}, u32[]{:S(2)}) async-start(bf16[8,64,1024]{2,1,0:T(8,128)(2,1)} %bitcast.232), calls=%async_computation.2 | async-start | bytes 2097152 | tf_op jit(solution)/shard_map/all_to_all | solution.py:190
  148.7 29.7 %all-to-all-start.1 = ((bf16[8,64,1024]{2,1,0:T(8,128)(2,1)}), bf16[8,64,1024]{2,1,0:T(8,128)(2,1)}, u32[]{:S(2)}, u32[]{:S(2)}) async-start(bf16[8,64,1024]{2,1,0:T(8,128)(2,1)} %fusion.47), calls=%async_computation.1 | async-start | bytes 2097152 | tf_op jit(solution)/shard_map/all_to_all | solution.py:160
  178.4 33.6 %all-to-all-start.3 = ((bf16[8,64,1024]{2,1,0:T(8,128)(2,1)}), bf16[8,64,1024]{2,1,0:T(8,128)(2,1)}, u32[]{:S(2)}, u32[]{:S(2)}) async-start(bf16[8,64,1024]{2,1,0:T(8,128)(2,1)} %fusion.44), calls=%async_computation.3 | async-start | bytes 2097152 | tf_op jit(solution)/shard_map/all_to_all | solution.py:211
  182.6 132.5 %reduce-scatter.12.cloned.1.call-start = ((), (), s32[]{:S(2)}) async-start(), calls=%async_computation.13 | async-start | bytes 5242880 | tf_op jit(solution)/shard_map/reduce_scatter | solution.py:267
  197.4 10.9 copy-start.14
  215.7 8.7 copy-start.20
  215.7 8.7 copy-start.23
  252.8 11.8 copy-start.13
  270.3 136.8 %reduce-scatter.16.cloned.1.call-start = ((), (), s32[]{:S(2)}) async-start(), calls=%async_computation.15 | async-start | bytes 4718592 | tf_op jit(solution)/shard_map/reduce_scatter | solution.py:277
  273.1 419.4 %reduce-scatter.20.cloned.1.call-start = ((), (), s32[]{:S(2)}) async-start(), calls=%async_computation.17 | async-start | bytes 18874368 | tf_op jit(solution)/shard_map/reduce_scatter | solution.py:279
  285.0 693.3 %reduce-scatter.18.cloned.1.call-start = ((), (), s32[]{:S(2)}) async-start(), calls=%async_computation.16 | async-start | bytes 18874368 | tf_op jit(solution)/shard_map/reduce_scatter | solution.py:278
  295.8 19.3 %copy-start.9 = (bf16[1,256,1024]{2,1,0:T(8,128)(2,1)S(1)}, bf16[1,256,1024]{2,1,0:T(8,128)(2,1)}, u32[]{:S(2)}) copy-start(bf16[1,256,1024]{2,1,0:T(8,128)(2,1)} %param.14) | copy-start | bytes 1572868
  295.8 19.3 %copy-start.25 = (f32[1024]{0:T(1024)S(1)}, f32[1024]{0:T(1024)}, u32[]{:S(2)}) copy-start(f32[1024]{0:T(1024)} %copy-done.24) | copy-start | bytes 12292
  295.8 19.3 %copy-start.29 = (f32[256]{0:T(256)S(1)}, f32[256]{0:T(256)}, u32[]{:S(2)}) copy-start(f32[256]{0:T(256)} %copy-done.28) | copy-start | bytes 3076
  295.8 19.3 %copy-start.32 = (f32[256]{0:T(256)S(1)}, f32[256]{0:T(256)}, u32[]{:S(2)}) copy-start(f32[256]{0:T(256)} %copy-done.31) | copy-start | bytes 3076
  295.8 892.5 %reduce-scatter.14.cloned.1.call-start = ((), (), s32[]{:S(2)}) async-start(), calls=%async_computation.14 | async-start | bytes 14155776 | tf_op jit(solution)/shard_map/reduce_scatter | solution.py:276
  322.9 930.4 %reduce-scatter.28.cloned.1.call-start = ((), (), s32[]{:S(2)}) async-start(), calls=%async_computation.22 | async-start | bytes 589824
  324.1 985.7 %reduce-scatter.22.cloned.1.call-start = ((), (), s32[]{:S(2)}) async-start(), calls=%async_computation.18 | async-start | bytes 36864 | tf_op jit(solution)/shard_map/reduce_scatter | solution.py:280
  325.0 1058.5 %reduce-scatter.26.cloned.1.call-start = ((), (), s32[]{:S(2)}) async-start(), calls=%async_computation.20 | async-start | bytes 10485760 | tf_op jit(solution)/shard_map/reduce_scatter | solution.py:217
  338.4 1119.2 %reduce-scatter.24.cloned.1.call-start = ((), (), s32[]{:S(2)}) async-start(), calls=%async_computation.19 | async-start | bytes 10485760 | tf_op jit(solution)/shard_map/reduce_scatter | solution.py:214
  348.9 841.7 %copy-start.35 = (u32[32]{0:T(128)S(1)}, u32[32]{0:T(128)}, u32[]{:S(2)}) copy-start(u32[32]{0:T(128)} %constant.122) | copy-start | bytes 388
  348.9 1181.0 %all-reduce.7.cloned.1.call-start = ((), (), s32[]{:S(2)}) async-start(), calls=%async_computation.23 | async-start | bytes 6291456 | tf_op jit(solution)/shard_map/psum | solution.py:287
  1457.6 81.0 %copy-start.1 = (bf16[1024,1024]{1,0:T(8,128)(2,1)S(1)}, bf16[1024,1024]{1,0:T(8,128)(2,1)}, u32[]{:S(2)}) copy-start(bf16[1024,1024]{1,0:T(8,128)(2,1)} %param.18) | copy-start | bytes 6291460
  (21 other events, 84.1 us)
Sparse Core Ops, SparseCore 0:
  17.9 37.1 all-gather.2
  270.4 44.6 reduce-scatter.11
  319.2 87.8 reduce-scatter.15
  410.7 281.7 reduce-scatter.19
  696.6 281.6 reduce-scatter.17
  981.8 206.4 reduce-scatter.13
  1192.2 61.0 reduce-scatter.27
  1257.3 52.4 reduce-scatter.21
  1312.6 70.8 reduce-scatter.25
  1385.9 71.6 reduce-scatter.23
  1460.9 69.0 all-reduce.6
where the time goes:
time: 1560 us; the launch traced here: 1550 us
  waiting for transfers between devices  1200 us (77%)
  matrix products  176 us (11%)
  other arithmetic  61.6 us (4%)
  local copies, waits for them, and re-layouts  37.4 us (2%)
  starting transfers between devices  28.5 us (2%)
  blocking collectives  25.8 us (2%)
    reduce_scatter x1, waiting for transfers between devices, per_device(): lax.psum_scatter(grad_fc2, 'wide', scatter_dimension=0, tiled=True)  284 us
    reduce_scatter x1, waiting for transfers between devices, per_device(): lax.psum_scatter(grad_fc1, 'wide', scatter_dimension=0, tiled=True)  283 us
    reduce_scatter x1, waiting for transfers between devices, per_device(): lax.psum_scatter(grad_qkv, 'wide', scatter_dimension=0, tiled=True)  207 us
    reduce_scatter x1, waiting for transfers between devices, per_device(): lax.psum_scatter(grad_expert_in.astype(jnp.bfloat16), 'narrow', scatter_d...  70 us
    psum x1, waiting for transfers between devices, per_device(): lax.psum(part_qkv.astype(jnp.bfloat16), 'narrow').astype(jnp.float32)  68.2 us
    unnamed x12, waiting for transfers between devices  61.5 us
    reduce_scatter x1, waiting for transfers between devices, per_device(): lax.psum_scatter(grad_out, 'wide', scatter_dimension=0, tiled=True)  57.9 us
    reduce_scatter x1, waiting for transfers between devices, per_device(): lax.psum_scatter(grad_router, 'wide', scatter_dimension=0, tiled=True)  55.7 us
  transfers between devices with their start and end apart: 15, of which 14 were waited for; matrix products, arithmetic and copies ran while one was open for 10% of the time, Pallas kernels for 0%

commit v1 on v0

v1 whole, which is shorter than its diff:
```python
import functools

import jax
import jax.numpy as jnp
from jax import lax
from jax.experimental import pallas as pl
from jax.experimental.pallas import tpu as pltpu
from jax.sharding import PartitionSpec as P

HEAD_DIM = 64
PAIR = 2 * HEAD_DIM
EPSILON = 1e-05
NEGATIVE_FILL = -1e30
VMEM_BYTES = 56 * 1024 * 1024
BF16 = jnp.bfloat16
F32 = jnp.float32


def normalize(values, gain):
    centred = values - jnp.mean(values, axis=-1, keepdims=True)
    spread = lax.rsqrt(jnp.mean(centred * centred, axis=-1, keepdims=True) + EPSILON)
    scaled = centred * spread
    return (scaled * gain, scaled, spread)


def normal_back(incoming, scaled, spread, gain):
    inner = incoming * gain
    return spread * (
        inner
        - jnp.mean(inner, axis=-1, keepdims=True)
        - scaled * jnp.mean(inner * scaled, axis=-1, keepdims=True)
    )


def dot(left, right, left_dim, right_dim):
    return lax.dot_general(
        left, right, (((left_dim,), (right_dim,)), ((), ())), preferred_element_type=F32
    )


def plain(left, right):
    return dot(left, right, 1, 0)


def across(left, right):
    return dot(left, right, 0, 0)


def beside(left, right):
    return dot(left, right, 1, 1)


def swap(values, axis, bit):
    size = lax.axis_size(axis)
    return lax.ppermute(values, axis, [(i, i ^ bit) for i in range(size)])


def x_bits():
    bits, bit = [], 2
    while bit < lax.axis_size("narrow"):
        bits.append(bit)
        bit *= 2
    return bits


def gather_pieces(values):
    pieces = [values]
    for bit in x_bits():
        pieces = pieces + [swap(piece, "narrow", bit) for piece in pieces]
    return pieces + [swap(piece, "narrow", 1) for piece in pieces]


def add_to_bf16(left, right):
    return (left.astype(F32) + right.astype(F32)).astype(BF16)


def scatter_addends(mine, other, rows):
    arrived = swap(other, "narrow", 1)
    bits = list(reversed(x_bits()))
    for bit in bits:
        half = mine.shape[0] // 2
        gone = add_to_bf16(mine[half:], arrived[half:])
        if bit == bits[-1]:
            return [mine, arrived, swap(gone, "narrow", bit)]
        mine, arrived = add_to_bf16(mine[:half], arrived[:half]), swap(gone, "narrow", bit)
    return [mine, arrived]


def natural_block(ids_ref, place, count):
    spots = count // 2
    return ids_ref[0] ^ (2 * (place % spots) + place // spots)


def natural_rows(ids_ref, place, count, rows):
    return pl.ds(pl.multiple_of(natural_block(ids_ref, place, count) * rows, rows), rows)


def params(steps=0):
    if steps:
        return pltpu.CompilerParams(
            vmem_limit_bytes=VMEM_BYTES, dimension_semantics=("arbitrary",) * steps
        )
    return pltpu.CompilerParams(vmem_limit_bytes=VMEM_BYTES)


def cost(flops, moved, curves=0):
    return pl.CostEstimate(flops=flops, bytes_accessed=moved, transcendentals=curves)


def in_vmem():
    return pl.BlockSpec(memory_space=pltpu.VMEM)


def in_smem():
    return pl.BlockSpec(memory_space=pltpu.SMEM)


def heads_kernel(ids_ref, *refs):
    *piece_refs, weight_ref, out_ref = refs
    count, rows = len(piece_refs), piece_refs[0].shape[0]
    for place, piece_ref in enumerate(piece_refs):
        out_ref[natural_rows(ids_ref, place, count, rows), :] = plain(
            piece_ref[...], weight_ref[...]
        ).astype(BF16)


def to_heads(ids, pieces, w_qkv):
    count = len(pieces)
    rows, width = pieces[0].shape
    part = width // count
    whole = pl.BlockSpec((rows, width), lambda j, s: (0, 0))
    return pl.pallas_call(
        heads_kernel,
        grid_spec=pltpu.PrefetchScalarGridSpec(
            num_scalar_prefetch=1,
            grid=(3,),
            in_specs=[whole] * count
            + [pl.BlockSpec((width, part), lambda j, s: (0, j * count + s[0]))],
            out_specs=pl.BlockSpec((count * rows, part), lambda j, s: (0, j)),
        ),
        out_shape=jax.ShapeDtypeStruct((count * rows, 3 * part), BF16),
        compiler_params=params(1),
        cost_estimate=cost(6 * count * rows * width * part, 2 * width * (count * rows + 3 * part)),
        name="to_heads",
    )(ids, *pieces, w_qkv)


def from_heads_kernel(count, ids_ref, d_ref, *refs):
    *weight_refs, mine_ref, other_ref = refs
    rows = d_ref.shape[0] // count
    weight = jnp.concatenate([ref[...] for ref in weight_refs], axis=1)
    for place in range(count):
        result = beside(d_ref[natural_rows(ids_ref, place, count, rows), :], weight)
        into = mine_ref if place < count // 2 else other_ref
        at = (place % (count // 2)) * rows
        into[at : at + rows, :] = result.astype(BF16)


def from_heads(ids, d_qkv, w_qkv):
    count = lax.axis_size("narrow")
    length, width = d_qkv.shape[0], w_qkv.shape[0]
    part = width // count
    half = pl.BlockSpec((length // 2, width), lambda i, s: (0, 0))
    place = lambda j: (lambda i, s: (0, j * count + s[0]))
    return pl.pallas_call(
        functools.partial(from_heads_kernel, count),
        grid_spec=pltpu.PrefetchScalarGridSpec(
            num_scalar_prefetch=1,
            grid=(1,),
            in_specs=[pl.BlockSpec(d_qkv.shape, lambda i, s: (0, 0))]
            + [pl.BlockSpec((width, part), place(j)) for j in range(3)],
            out_specs=[half, half],
        ),
        out_shape=[jax.ShapeDtypeStruct((length // 2, width), BF16)] * 2,
        compiler_params=params(1),
        cost_estimate=cost(6 * length * width * part, 2 * length * width * 2),
        name="from_heads",
    )(ids, d_qkv, w_qkv, w_qkv, w_qkv)


def block_bias(seg_row_ref, seg_col_ref, block, rows):
    keys = (block + 1) * rows
    key_pos = lax.broadcasted_iota(jnp.int32, (keys, rows), 0)
    query_pos = lax.broadcasted_iota(jnp.int32, (keys, rows), 1) + block * rows
    same = seg_col_ref[0:keys, :] == seg_row_ref[:, block * rows : (block + 1) * rows]
    return jnp.where((key_pos <= query_pos) & same, 0.0, NEGATIVE_FILL)


def soft_columns(keys, query, bias):
    scores = beside(keys, query) * (HEAD_DIM**-0.5) + bias
    weights = jnp.exp(scores - jnp.max(scores, axis=0, keepdims=True))
    return weights * (1.0 / jnp.sum(weights, axis=0, keepdims=True))


def attend_kernel(count, seg_row_ref, seg_col_ref, qkv_ref, out_ref):
    width = out_ref.shape[1]
    rows = out_ref.shape[0] // count
    lane = lax.broadcasted_iota(jnp.int32, (rows, PAIR), 1)
    for block in range(count):
        span = slice(block * rows, (block + 1) * rows)
        seen = slice(0, (block + 1) * rows)
        bias = block_bias(seg_row_ref, seg_col_ref, block, rows)
        for pair in range(width // PAIR):
            columns = slice(pair * PAIR, (pair + 1) * PAIR)
            query = qkv_ref[span, columns]
            keys = qkv_ref[seen, width + pair * PAIR : width + (pair + 1) * PAIR]
            values = qkv_ref[seen, 2 * width + pair * PAIR : 2 * width + (pair + 1) * PAIR]
            halves = []
            for head in range(2):
                here = (lane // HEAD_DIM) == head
                probs = soft_columns(keys, jnp.where(here, query, 0), bias).astype(BF16)
                mixed = across(values, probs)
                halves.append(mixed[head * HEAD_DIM : (head + 1) * HEAD_DIM])
            out_ref[span, columns] = jnp.concatenate(halves, axis=0).T.astype(BF16)


def attend_back_kernel(count, seg_row_ref, seg_col_ref, qkv_ref, d_ref, out_ref, total_ref):
    width = d_ref.shape[1]
    rows = d_ref.shape[0] // count
    scale = HEAD_DIM**-0.5
    lane = lax.broadcasted_iota(jnp.int32, (rows, PAIR), 1)
    total_ref[...] = jnp.zeros_like(total_ref)
    for block in range(count):
        span = slice(block * rows, (block + 1) * rows)
        seen = slice(0, (block + 1) * rows)
        bias = block_bias(seg_row_ref, seg_col_ref, block, rows)
        for pair in range(width // PAIR):
            columns = slice(pair * PAIR, (pair + 1) * PAIR)
            key_columns = slice(width + pair * PAIR, width + (pair + 1) * PAIR)
            value_columns = slice(2 * width + pair * PAIR, 2 * width + (pair + 1) * PAIR)
            query = qkv_ref[span, columns]
            keys = qkv_ref[seen, key_columns]
            values = qkv_ref[seen, value_columns]
            incoming = d_ref[span, columns]
            halves = []
            for head in range(2):
                here = (lane // HEAD_DIM) == head
                own_query = jnp.where(here, query, 0)
                own_incoming = jnp.where(here, incoming, 0)
                probs = soft_columns(keys, own_query, bias)
                d_probs = beside(values, own_incoming)
                mean = jnp.sum(probs * d_probs, axis=0, keepdims=True)
                d_scores = (probs * (d_probs - mean)).astype(BF16)
                total_ref[seen, width + pair * PAIR : width + (pair + 1) * PAIR] += plain(
                    probs.astype(BF16), own_incoming
                )
                total_ref[seen, columns] += plain(d_scores, own_query)
                mixed = across(keys, d_scores)
                halves.append(mixed[head * HEAD_DIM : (head + 1) * HEAD_DIM])
            out_ref[span, columns] = (jnp.concatenate(halves, axis=0).T * scale).astype(BF16)
    out_ref[:, width : 2 * width] = (total_ref[:, :width] * scale).astype(BF16)
    out_ref[:, 2 * width :] = total_ref[:, width:].astype(BF16)


def attention_cost(length, width, matmuls):
    return cost(
        matmuls * length * length * width,
        length * width * 16,
        length * length * width // HEAD_DIM,
    )


def attend(seg_row, seg_col, qkv):
    length, width = qkv.shape[0], qkv.shape[1] // 3
    return pl.pallas_call(
        functools.partial(attend_kernel, lax.axis_size("narrow")),
        out_shape=jax.ShapeDtypeStruct((length, width), BF16),
        in_specs=[in_vmem()] * 3,
        out_specs=in_vmem(),
        compiler_params=params(),
        cost_estimate=attention_cost(length, width, 4),
        name="attend",
    )(seg_row, seg_col, qkv)


def attend_back(seg_row, seg_col, qkv, d_attended):
    length, width = d_attended.shape
    return pl.pallas_call(
        functools.partial(attend_back_kernel, lax.axis_size("narrow")),
        out_shape=jax.ShapeDtypeStruct(qkv.shape, BF16),
        in_specs=[in_vmem()] * 4,
        out_specs=in_vmem(),
        scratch_shapes=[pltpu.VMEM((length, 2 * width), F32)],
        compiler_params=params(),
        cost_estimate=attention_cost(length, width, 10),
        name="attend_back",
    )(seg_row, seg_col, qkv, d_attended)


def softmax_lanes(logits, here):
    weights = jnp.where(here, jnp.exp(logits - jnp.max(jnp.where(here, logits, NEGATIVE_FILL), axis=-1, keepdims=True)), 0.0)
    return weights * (1.0 / jnp.sum(weights, axis=-1, keepdims=True))


def norm_rows(values):
    centred = values - jnp.mean(values, axis=-1, keepdims=True)
    spread = lax.rsqrt(jnp.mean(centred * centred, axis=-1, keepdims=True) + EPSILON)
    return (centred * spread, spread)


def pick(gates, lane, index):
    return jnp.sum(jnp.where(lane == index, gates, 0.0), axis=-1, keepdims=True)


def middle_kernel(
    experts,
    capacity,
    parts_ref,
    w_out_ref,
    tokens_ref,
    d_ref,
    gain_ref,
    logit_ref,
    routes_ref,
    mid_ref,
    second_ref,
    d_dense_ref,
    slots_ref,
    d_slots_ref,
    to_slot_ref,
    gates_ref,
):
    count, rows, part = parts_ref.shape
    attended = jnp.concatenate([parts_ref[k] for k in range(count)], axis=1)
    mid = tokens_ref[...].astype(F32) + plain(attended, w_out_ref[...])
    mid_ref[...] = mid
    second = (norm_rows(mid)[0] * gain_ref[...].astype(F32)).astype(BF16)
    second_ref[...] = second
    logits = plain(second, logit_ref[...])
    lane = lax.broadcasted_iota(jnp.int32, logits.shape, 1)
    route_probs = softmax_lanes(logits, lane < experts)
    mixing = softmax_lanes(logits, (lane >= experts) & (lane < experts + 2))
    gates_ref[...] = route_probs + mixing
    routes = routes_ref[...]
    chosen = lane == routes
    gate = jnp.sum(jnp.where(chosen, route_probs, 0.0), axis=-1, keepdims=True)
    d_output = d_ref[...].astype(F32)
    d_dense_ref[...] = (d_output * pick(mixing, lane, experts)).astype(BF16)
    d_expert = (d_output * pick(mixing, lane, experts + 1) * gate).astype(BF16)
    before = (
        lax.broadcasted_iota(jnp.int32, (rows, rows), 1)
        < lax.broadcasted_iota(jnp.int32, (rows, rows), 0)
    ).astype(F32).astype(BF16)
    earlier = plain(before, chosen.astype(F32).astype(BF16))
    position = jnp.sum(jnp.where(chosen, earlier, 0.0), axis=-1, keepdims=True)
    slot = routes * capacity + position.astype(jnp.int32)
    slots = experts * capacity
    to_slot = (
        (lax.broadcasted_iota(jnp.int32, (rows, slots), 1) == slot).astype(F32).astype(BF16)
    )
    to_slot_ref[...] = to_slot
    slots_ref[...] = across(to_slot, second).astype(BF16)
    d_slots_ref[...] = across(to_slot, d_expert).astype(BF16)


def middle(parts, w_out, tokens, d_output, gain, logit_weight, routes, experts, capacity):
    rows, width = tokens.shape
    slots = experts * capacity
    lanes = logit_weight.shape[1]
    return pl.pallas_call(
        functools.partial(middle_kernel, experts, capacity),
        out_shape=[
            jax.ShapeDtypeStruct((rows, width), F32),
            jax.ShapeDtypeStruct((rows, width), BF16),
            jax.ShapeDtypeStruct((rows, width), BF16),
            jax.ShapeDtypeStruct((slots, width), BF16),
            jax.ShapeDtypeStruct((slots, width), BF16),
            jax.ShapeDtypeStruct((rows, slots), BF16),
            jax.ShapeDtypeStruct((rows, lanes), F32),
        ],
        in_specs=[in_vmem()] * 7,
        out_specs=[in_vmem()] * 7,
        compiler_params=params(),
        cost_estimate=cost(2 * rows * width * (width + 2 * slots), 2 * width * (width + 8 * rows)),
        name="middle",
    )(parts, w_out, tokens, d_output, gain, logit_weight, routes)


def merge_kernel(
    experts,
    results,
    back_ref,
    d_back_ref,
    to_slot_ref,
    gates_ref,
    routes_ref,
    mid_ref,
    second_ref,
    d_ref,
    gain_ref,
    logit_ref,
    w_out_ref,
    *refs,
):
    sums, outs = refs[: 2 * results], refs[2 * results :]
    output_ref, d_mid_ref, d_attn_ref, d_attended_ref, small_ref = outs
    to_slot = to_slot_ref[...]
    expert_result = plain(to_slot, back_ref[...])
    d_second = plain(to_slot, d_back_ref[...])
    dense_result = sums[0][...].astype(F32)
    for ref in sums[1:results]:
        dense_result = dense_result + ref[...].astype(F32)
    for ref in sums[results:]:
        d_second = d_second + ref[...].astype(F32)
    gates = gates_ref[...]
    lane = lax.broadcasted_iota(jnp.int32, gates.shape, 1)
    chosen = lane == routes_ref[...]
    gate = pick(gates, lane, routes_ref[...])
    mix_dense, mix_expert = pick(gates, lane, experts), pick(gates, lane, experts + 1)
    mid = mid_ref[...]
    d_output = d_ref[...].astype(F32)
    output_ref[...] = (
        mid + mix_dense * dense_result + mix_expert * gate * expert_result
    ).astype(BF16)
    on_dense = jnp.sum(d_output * dense_result, axis=-1, keepdims=True)
    on_expert = jnp.sum(d_output * expert_result, axis=-1, keepdims=True)
    mean = mix_dense * on_dense + mix_expert * (gate * on_expert)
    d_mix = gates * (jnp.where(lane == experts, on_dense, gate * on_expert) - mean)
    d_route = gates * (chosen.astype(F32) - gate) * (mix_expert * on_expert)
    d_logits = jnp.where(
        lane < experts, d_route, jnp.where(lane < experts + 2, d_mix, 0.0)
    ).astype(BF16)
    d_second = d_second + beside(d_logits, logit_ref[...])
    scaled, spread = norm_rows(mid)
    d_gain = jnp.sum(d_second * scaled, axis=0, keepdims=True)
    d_mid = d_output + normal_back(d_second, scaled, spread, gain_ref[...].astype(F32))
    d_mid_ref[...] = d_mid
    d_attn = d_mid.astype(BF16)
    d_attended = beside(d_attn, w_out_ref[...]).astype(BF16)
    count, rows, part = d_attn_ref.shape
    for block in range(count):
        d_attn_ref[block] = d_attn[:, block * part : (block + 1) * part]
        d_attended_ref[block] = d_attended[:, block * part : (block + 1) * part]
    small = across(second_ref[...], d_logits)
    column = jnp.broadcast_to(d_gain, (small.shape[1], small.shape[0])).T
    small_lane = lax.broadcasted_iota(jnp.int32, small.shape, 1)
    small_ref[...] = jnp.where(small_lane == experts + 2, column, small).astype(BF16)


def merge(back, d_back, to_slot, gates, routes, mid, second, d_output, gain, logit_weight, w_out,
          dense_sums, d_second_sums, experts, count):
    rows, width = mid.shape
    part = width // count
    slots = to_slot.shape[1]
    lanes = logit_weight.shape[1]
    whole = lambda v: pl.BlockSpec(v.shape, lambda i: (0,) * v.ndim)
    top = pl.BlockSpec((rows, width), lambda i: (0, 0))
    blocks = pl.BlockSpec((count, rows, part), lambda i: (0, 0, 0))
    given = (back, d_back, to_slot, gates, routes, mid, second, d_output, gain, logit_weight, w_out)
    return pl.pallas_call(
        functools.partial(merge_kernel, experts, len(dense_sums)),
        grid=(1,),
        out_shape=[
            jax.ShapeDtypeStruct((rows, width), BF16),
            jax.ShapeDtypeStruct((rows, width), F32),
            jax.ShapeDtypeStruct((count, rows, part), BF16),
            jax.ShapeDtypeStruct((count, rows, part), BF16),
            jax.ShapeDtypeStruct((width, lanes), BF16),
        ],
        in_specs=[whole(v) for v in given] + [top] * (2 * len(dense_sums)),
        out_specs=[top, top, blocks, blocks, pl.BlockSpec((width, lanes), lambda i: (0, 0))],
        compiler_params=params(1),
        cost_estimate=cost(2 * rows * width * (width + 2 * slots), 2 * width * (width + 16 * rows)),
        name="merge",
    )(*given, *dense_sums, *d_second_sums)


def finish_kernel(tokens_ref, gain_ref, d_mid_ref, *refs):
    *sum_refs, out_ref = refs
    incoming = sum_refs[0][...].astype(F32)
    for ref in sum_refs[1:]:
        incoming = incoming + ref[...].astype(F32)
    scaled, spread = norm_rows(tokens_ref[...].astype(F32))
    out_ref[...] = d_mid_ref[...] + normal_back(
        incoming, scaled, spread, gain_ref[...].astype(F32)
    )


def finish(tokens, gain, d_mid, sums):
    rows, width = tokens.shape
    top = pl.BlockSpec((rows, width), lambda i: (0, 0))
    return pl.pallas_call(
        finish_kernel,
        grid=(1,),
        out_shape=jax.ShapeDtypeStruct((rows, width), F32),
        in_specs=[top, pl.BlockSpec((1, width), lambda i: (0, 0)), top] + [top] * len(sums),
        out_specs=top,
        compiler_params=params(1),
        cost_estimate=cost(20 * rows * width, 20 * rows * width),
        name="finish",
    )(tokens, gain, d_mid, *sums)


def whole_rows(refs):
    return jnp.concatenate([ref[...] for ref in refs], axis=0)


def whole_columns(refs):
    return jnp.concatenate([ref[...] for ref in refs], axis=1)


def row_chunks(refs, size):
    chunks, at = [], 0
    for ref in refs:
        for start in range(0, ref.shape[0], size):
            chunks.append((ref, start, at + start))
        at += ref.shape[0]
    return chunks


CHUNK = 256


def write_halves(total_ref, mine_ref, other_ref):
    @pl.when(pl.program_id(0) == pl.num_programs(0) - 1)
    def _():
        half = mine_ref.shape[0]
        mine_ref[...] = total_ref[:half, :].astype(BF16)
        other_ref[...] = total_ref[half:, :].astype(BF16)


def clear_first(total_ref):
    @pl.when(pl.program_id(0) == 0)
    def _():
        total_ref[...] = jnp.zeros_like(total_ref)


def forward_kernel(pieces, slices, ids_ref, *refs):
    piece_refs, refs = refs[:pieces], refs[pieces:]
    in_refs, out_refs, refs = refs[:slices], refs[slices : 2 * slices], refs[2 * slices :]
    hidden_ref, slope_ref, mine_ref, other_ref, total_ref = refs
    clear_first(total_ref)
    weight_in, weight_out = whole_columns(in_refs), whole_rows(out_refs)
    chunks = row_chunks(piece_refs, CHUNK)
    first_dot = lambda c: plain(c[0][c[1] : c[1] + CHUNK, :], weight_in)
    pre = first_dot(chunks[0])
    for index, (_, _, at) in enumerate(chunks):
        later = first_dot(chunks[index + 1]) if index + 1 < len(chunks) else None
        square = pre * pre
        curve = jnp.tanh(pre * (0.7978845608 + (0.7978845608 * 0.044715) * square))
        half = 0.5 + 0.5 * curve
        hidden = (pre * half).astype(BF16)
        slope = half + (0.5 * pre) * (1.0 - curve * curve) * (
            0.7978845608 + (3.0 * 0.7978845608 * 0.044715) * square
        )
        hidden_ref[at : at + CHUNK, :] = hidden
        slope_ref[at : at + CHUNK, :] = slope.astype(BF16)
        total_ref[at : at + CHUNK, :] += plain(hidden, weight_out)
        pre = later
    write_halves(total_ref, mine_ref, other_ref)


def backward_kernel(pieces, slices, ids_ref, *refs):
    piece_refs, refs = refs[:pieces], refs[pieces:]
    in_refs, out_refs, refs = refs[:slices], refs[slices : 2 * slices], refs[2 * slices :]
    slope_ref, d_pre_ref, mine_ref, other_ref, total_ref = refs
    clear_first(total_ref)
    weight_in, weight_out = whole_columns(in_refs), whole_rows(out_refs)
    chunks = row_chunks(piece_refs, CHUNK)
    first_dot = lambda c: beside(c[0][c[1] : c[1] + CHUNK, :], weight_out)
    d_hidden = first_dot(chunks[0])
    for index, (_, _, at) in enumerate(chunks):
        later = first_dot(chunks[index + 1]) if index + 1 < len(chunks) else None
        d_pre = (d_hidden * slope_ref[at : at + CHUNK, :].astype(F32)).astype(BF16)
        d_pre_ref[at : at + CHUNK, :] = d_pre
        total_ref[at : at + CHUNK, :] += beside(d_pre, weight_in)
        d_hidden = later
    write_halves(total_ref, mine_ref, other_ref)


def feed(kernel, name, ids, pieces, weight_in, weight_out, units, places, block, slope=None):
    width = pieces[0].shape[1]
    count = sum(piece.shape[0] for piece in pieces)
    size = block // len(places)
    unit_spec = pl.BlockSpec((count, block), lambda f, s: (0, f))
    half_spec = pl.BlockSpec((count // 2, width), lambda f, s: (0, 0))
    in_places = [(lambda f, s, p=p: (0, p(f, s))) for p in places]
    out_places = [(lambda f, s, p=p: (p(f, s), 0)) for p in places]
    in_specs = (
        [pl.BlockSpec(piece.shape, lambda f, s: (0, 0)) for piece in pieces]
        + [pl.BlockSpec((width, size), p) for p in in_places]
        + [pl.BlockSpec((size, width), p) for p in out_places]
    )
    given = [*pieces] + [weight_in] * len(places) + [weight_out] * len(places)
    if slope is not None:
        in_specs.append(unit_spec)
        given.append(slope)
    unit_outs = 2 if slope is None else 1
    return pl.pallas_call(
        functools.partial(kernel, len(pieces), len(places)),
        grid_spec=pltpu.PrefetchScalarGridSpec(
            num_scalar_prefetch=1,
            grid=(units // block,),
            in_specs=in_specs,
            out_specs=[unit_spec] * unit_outs + [half_spec] * 2,
            scratch_shapes=[pltpu.VMEM((count, width), F32)],
        ),
        out_shape=[jax.ShapeDtypeStruct((count, units), BF16)] * unit_outs
        + [jax.ShapeDtypeStruct((count // 2, width), BF16)] * 2,
        compiler_params=params(1),
        cost_estimate=cost(
            4 * count * width * units,
            2 * (2 * count * width + 2 * width * units + 2 * count * units),
            count * units,
        ),
        name=name,
    )(ids, *given)


def grad_kernel(lefts, rights, ids_ref, *refs):
    left = whole_rows(refs[:lefts])
    right = whole_rows(refs[lefts : lefts + rights])
    total = across(left, right)
    for ref in refs[lefts + rights : -1]:
        total = total + ref[...].astype(F32)
    refs[-1][...] = total.astype(refs[-1].dtype)


def grad(name, ids, lefts, rights, rows, steps, left_place, columns=None, right_place=None,
         added=None, added_place=None, out=None, out_place=None, dtype=BF16):
    depth = sum(v.shape[0] for v in lefts)
    columns = columns or rights[0].shape[1]
    right_place = right_place or (lambda i, s: 0)
    out_place = out_place or (lambda i, s: (i, 0))
    out = out or (rows * steps, columns)
    in_specs = [
        pl.BlockSpec((v.shape[0], rows), lambda i, s: (0, left_place(i, s))) for v in lefts
    ] + [pl.BlockSpec((v.shape[0], columns), lambda i, s: (0, right_place(i, s))) for v in rights]
    given = [*lefts, *rights]
    if added is not None:
        in_specs.append(pl.BlockSpec((rows, columns), added_place or out_place))
        given.append(added)
    return pl.pallas_call(
        functools.partial(grad_kernel, len(lefts), len(rights)),
        grid_spec=pltpu.PrefetchScalarGridSpec(
            num_scalar_prefetch=1,
            grid=(steps,),
            in_specs=in_specs,
            out_specs=pl.BlockSpec((rows, columns), out_place),
        ),
        out_shape=jax.ShapeDtypeStruct(out, dtype),
        compiler_params=params(1),
        cost_estimate=cost(
            2 * depth * rows * steps * columns,
            2 * (depth * (rows * steps + columns) + 2 * rows * steps * columns),
        ),
        name=name,
    )(ids, *given)


def feed_grads_kernel(pieces, ids_ref, hidden_ref, d_pre_ref, *refs):
    row_refs, d_refs, (keep_ref, gone_ref) = refs[:pieces], refs[pieces:-2], refs[-2:]
    part = d_pre_ref.shape[1]
    half = keep_ref.shape[0]
    swapped = (ids_ref[3] & 1) == 1

    def put(total, columns):
        total = total.astype(BF16)
        keep_ref[:, columns] = jnp.where(swapped, total[half:], total[:half])
        gone_ref[:, columns] = jnp.where(swapped, total[:half], total[half:])

    put(across(whole_rows(row_refs), d_pre_ref[...]), slice(0, part))
    put(across(hidden_ref[...], whole_rows(d_refs)), slice(part, part + keep_ref.shape[1] - part))


def feed_grads(ids, rows, d_rows, hidden, d_pre):
    count, width = rows[0].shape
    length, part = d_pre.shape
    steps = lax.axis_size("wide") // 2
    fixed = lambda v: pl.BlockSpec(v.shape, lambda i, s: (0, 0))
    out = jax.ShapeDtypeStruct((width // 2, part + width), BF16)
    out_spec = pl.BlockSpec((width // steps // 2, part + width), lambda i, s: (i, 0))
    return pl.pallas_call(
        functools.partial(feed_grads_kernel, len(rows)),
        grid_spec=pltpu.PrefetchScalarGridSpec(
            num_scalar_prefetch=1,
            grid=(steps,),
            in_specs=[pl.BlockSpec((length, part // steps), lambda i, s: (0, i)), fixed(d_pre)]
            + [pl.BlockSpec((count, width // steps), lambda i, s: (0, i))] * len(rows)
            + [fixed(v) for v in d_rows],
            out_specs=[out_spec, out_spec],
        ),
        out_shape=[out, out],
        compiler_params=params(1),
        cost_estimate=cost(4 * length * width * part, 2 * (4 * length * width + 2 * width * part)),
        name="feed_grads",
    )(ids, hidden, d_pre, *rows, *d_rows)


def heads_grad_kernel(count, ids_ref, *refs):
    piece_refs, (d_ref, out_sum_ref, small_ref, out_ref) = refs[:count], refs[count:]
    rows = piece_refs[0].shape[0]
    right = jnp.concatenate(
        [d_ref[natural_rows(ids_ref, place, count, rows), :] for place in range(count)], axis=0
    )
    triple, part = right.shape[1], out_sum_ref.shape[1]
    out_ref[:, :triple] = across(whole_rows(piece_refs), right).astype(BF16)
    out_ref[:, triple : triple + part] = out_sum_ref[...]
    out_ref[:, triple + part :] = small_ref[...]


def heads_grad(ids, pieces, d_qkv, out_sum, small):
    rows, width = pieces[0].shape
    length, triple = d_qkv.shape
    part, lanes = out_sum.shape[1], small.shape[1]
    block = 256
    return pl.pallas_call(
        functools.partial(heads_grad_kernel, len(pieces)),
        grid_spec=pltpu.PrefetchScalarGridSpec(
            num_scalar_prefetch=1,
            grid=(width // block,),
            in_specs=[pl.BlockSpec((rows, block), lambda i, s: (0, i))] * len(pieces)
            + [
                pl.BlockSpec(d_qkv.shape, lambda i, s: (0, 0)),
                pl.BlockSpec((block, part), lambda i, s: (i, 0)),
                pl.BlockSpec((block, lanes), lambda i, s: (i, 0)),
            ],
            out_specs=pl.BlockSpec((block, triple + part + lanes), lambda i, s: (i, 0)),
        ),
        out_shape=jax.ShapeDtypeStruct((width, triple + part + lanes), BF16),
        compiler_params=params(1),
        cost_estimate=cost(2 * length * width * triple, 4 * length * width),
        name="heads_grad",
    )(ids, *pieces, d_qkv, out_sum, small)


def out_grad_kernel(ids_ref, attended_ref, d_ref, mine_ref, other_ref):
    count, _, part = d_ref.shape
    spots = count // 2
    for place in range(count):
        total = across(attended_ref[0], d_ref[natural_block(ids_ref, place, count)])
        into = mine_ref if place < spots else other_ref
        at = (place % spots) * part
        into[:, at : at + part] = total.astype(BF16)


def out_grad(ids, attended, d_attn):
    count, rows, part = attended.shape
    out = jax.ShapeDtypeStruct((count * part, count * part // 2), BF16)
    out_spec = pl.BlockSpec((part, count * part // 2), lambda i, s: (i, 0))
    return pl.pallas_call(
        out_grad_kernel,
        grid_spec=pltpu.PrefetchScalarGridSpec(
            num_scalar_prefetch=1,
            grid=(count,),
            in_specs=[
                pl.BlockSpec((1, rows, part), lambda i, s: (i, 0, 0)),
                pl.BlockSpec(d_attn.shape, lambda i, s: (0, 0, 0)),
            ],
            out_specs=[out_spec, out_spec],
        ),
        out_shape=[out, out],
        compiler_params=params(1),
        cost_estimate=cost(2 * rows * (part * count) ** 2, 8 * (part * count) ** 2),
        name="out_grad",
    )(ids, attended, d_attn)


def scatter_columns(mine, other, columns):
    total = add_to_bf16(mine, swap(other, "narrow", 1))
    for bit in reversed(x_bits()):
        half = total.shape[1] // 2
        total = add_to_bf16(total[:, :half], swap(total[:, half:], "narrow", bit))
    return total


def put_feed_kernel(count, all_ref, first_out_ref, second_out_ref):
    held, width = all_ref.shape[1], second_out_ref.shape[1]
    part = all_ref.shape[2] - width
    for n in range(count):
        for w in range(part // held):
            at = (w * count + n) * held
            first_out_ref[:, at : at + held] = all_ref[n][:, w * held : (w + 1) * held].astype(F32)
        second_out_ref[n * held : (n + 1) * held, :] = all_ref[n][:, part:].astype(F32)


def put_feed(feed_all, width):
    count, held, both = feed_all.shape
    part = both - width
    return pl.pallas_call(
        functools.partial(put_feed_kernel, count),
        out_shape=[
            jax.ShapeDtypeStruct((held, count * part), F32),
            jax.ShapeDtypeStruct((count * held, width), F32),
        ],
        in_specs=[in_vmem()],
        out_specs=[in_vmem()] * 2,
        compiler_params=params(),
        cost_estimate=cost(0, 6 * count * held * both),
        name="put_feed",
    )(feed_all)


def put_heads_kernel(count, experts, ids_ref, *refs):
    piece_refs, refs = refs[:count], refs[count:]
    w_ref, gain_ref, grad_qkv_ref, grad_out_ref, router_ref, mix_ref, one_ref, two_ref = refs
    width = w_ref.shape[1] // 3
    part = width // count
    small = None
    for place in range(count):
        n = natural_block(ids_ref, place, count)
        for j in range(3):
            at = pl.multiple_of(j * width + n * part, part)
            grad_qkv_ref[:, pl.ds(at, part)] = piece_refs[place][
                :, j * part : (j + 1) * part
            ].astype(F32)
        at = pl.multiple_of(n * part, part)
        grad_out_ref[:, pl.ds(at, part)] = piece_refs[place][:, 3 * part : 4 * part].astype(F32)
        its = piece_refs[place][:, 4 * part :].astype(F32)
        small = its if small is None else small + its
    router_ref[...] = small[:, :experts]
    mix_ref[...] = small[:, experts : experts + 2]
    two_ref[...] = small.T[experts + 2 : experts + 3, :]
    weighed = jnp.sum(w_ref[...].astype(F32) * grad_qkv_ref[...], axis=1, keepdims=True)
    weighed = jnp.broadcast_to(weighed, small.shape).T[0:1, :]
    one_ref[...] = weighed / gain_ref[0].astype(F32)


def put_heads(ids, pieces, w_qkv, gain, experts):
    count = len(pieces)
    held = pieces[0].shape[0]
    width = w_qkv.shape[0]
    fixed = lambda shape: pl.BlockSpec(shape, lambda i, s: (0,) * len(shape))
    outs = [(held, 3 * width), (held, width), (held, experts), (held, 2), (1, held), (1, held)]
    return pl.pallas_call(
        functools.partial(put_heads_kernel, count, experts),
        grid_spec=pltpu.PrefetchScalarGridSpec(
            num_scalar_prefetch=1,
            grid=(1,),
            in_specs=[fixed(v.shape) for v in pieces]
            + [
                pl.BlockSpec((held, 3 * width), lambda i, s: (s[3], 0)),
                pl.BlockSpec((1, 1, held), lambda i, s: (s[3], 0, 0)),
            ],
            out_specs=[fixed(shape) for shape in outs],
        ),
        out_shape=[jax.ShapeDtypeStruct(shape, F32) for shape in outs],
        compiler_params=params(1),
        cost_estimate=cost(2 * held * 3 * width, 20 * held * width),
        name="put_heads",
    )(ids, *pieces, w_qkv, gain.reshape(width // held, 1, held))


def fill_kernel(ids_ref, half_ref, whole_ref, out_ref):
    out_ref[...] = half_ref[...].astype(F32)


def fill_other(ids, half, whole):
    rows, columns = half.shape
    spots = lax.axis_size("narrow") // 2
    quarter = columns // spots
    return pl.pallas_call(
        fill_kernel,
        grid_spec=pltpu.PrefetchScalarGridSpec(
            num_scalar_prefetch=1,
            grid=(spots,),
            in_specs=[
                pl.BlockSpec((rows, quarter), lambda i, s: (0, i)),
                pl.BlockSpec(memory_space=pl.ANY),
            ],
            out_specs=pl.BlockSpec((rows, quarter), lambda i, s: (0, 2 * i + 1 - s[1])),
        ),
        out_shape=jax.ShapeDtypeStruct(whole.shape, F32),
        input_output_aliases={2: 0},
        compiler_params=params(1),
        cost_estimate=cost(0, 6 * rows * columns),
        name="fill_other",
    )(ids, half, whole)


def wide_sum(values):
    return lax.psum_scatter(values, "wide", scatter_dimension=0, tiled=True)


def wide_sum_at_once(values):
    wide = lax.axis_size("wide")
    blocks = values.reshape(wide, values.shape[0] // wide, values.shape[1])
    arrived = lax.all_to_all(blocks, "wide", split_axis=0, concat_axis=0, tiled=True)
    return jnp.sum(arrived.astype(F32), axis=0).astype(BF16)


def narrow_all(values):
    return lax.all_gather(values, "narrow", axis=0, tiled=False)


def tied(value, *others):
    return lax.optimization_barrier((value, *others))[0]


def out_leaves(ids, d_rows, hidden):
    block = min(512, hidden.shape[1] // 2)
    per = hidden.shape[1] // 2 // block
    return grad("out_gone", ids, [hidden], d_rows, block, per, lambda i, s: (1 - s[2]) * per + i)


def in_leaves(ids, rows, d_pre):
    part = rows[0].shape[1] // 4
    return grad("in_gone", ids, rows, [d_pre], part, 2, lambda i, s: 2 * (1 - s[2]) + i)


def expert_grads(ids, rows, d_rows, hidden, d_pre, own, out_came, in_came, later):
    narrow = lax.axis_size("narrow")
    spots = narrow // 2
    width, shared = rows[0].shape[1], hidden.shape[1]
    quarter = shared // spots
    part = width // narrow
    if spots == 2:
        block = min(512, quarter)
        per = quarter // block
        hidden = tied(hidden, later)
        grad_out = grad("out_kept", ids, [hidden], d_rows, block, per,
                        lambda i, s: s[2] * per + i, added=out_came, dtype=F32)
        in_other = grad("in_other", ids, rows, [d_pre], part, 1,
                        lambda i, s: 2 * s[2] + 1 - s[1], added=in_came,
                        added_place=lambda i, s: (1 - s[1], 0))
        in_arrived = swap(in_other, "narrow", 1)
        in_kept = grad("in_kept", ids, rows, [d_pre], part, spots,
                       lambda i, s: 2 * s[2] + s[1], columns=quarter,
                       right_place=lambda i, s: i, added=in_came,
                       added_place=lambda i, s: (s[1], i),
                       out=(part, 2 * shared), out_place=lambda i, s: (0, 2 * i + s[1]),
                       dtype=F32)
        return fill_other(ids, in_arrived, in_kept), grad_out
    groups = [[2 * x + c for x in range(spots)] for c in range(2)]
    all_rows = jnp.concatenate(rows, axis=0)
    all_d_rows = jnp.concatenate(d_rows, axis=0)
    over_x = lambda v: lax.psum_scatter(
        v.astype(BF16), "narrow", scatter_dimension=0, axis_index_groups=groups, tiled=True
    )
    grad_out = over_x(across(hidden, all_d_rows)).astype(F32)
    in_sum = over_x(across(all_rows, d_pre)).reshape(2, part, shared)
    core = own & 1
    kept = lax.dynamic_index_in_dim(in_sum, core, 0, keepdims=False).astype(F32)
    gone = lax.dynamic_index_in_dim(in_sum, 1 - core, 0, keepdims=False)
    came = swap(gone, "narrow", 1).astype(F32)
    even = jnp.where(core == 0, kept, came).reshape(part, spots, 1, quarter)
    odd = jnp.where(core == 0, came, kept).reshape(part, spots, 1, quarter)
    grad_in = jnp.concatenate([even, odd], axis=2).reshape(part, 2 * shared)
    return grad_in, grad_out


def per_device(
    tokens,
    segments,
    routes,
    w_qkv,
    w_out,
    w_fc1,
    w_fc2,
    router,
    mix_weight,
    gain_one,
    gain_two,
    expert_in,
    expert_out,
    cotangent,
):
    rows, width = tokens.shape[1:]
    length = segments.shape[1]
    experts = router.shape[1]
    capacity = 2 * rows // experts
    narrow, wide = lax.axis_size("narrow"), lax.axis_size("wide")
    own = lax.axis_index("narrow")
    units = w_fc1.shape[1]
    part = width // narrow
    ids = jnp.stack([own, own & 1, own >> 1, lax.axis_index("wide")]).astype(jnp.int32)
    seg_row, seg_col = segments.reshape(1, length), segments.reshape(length, 1)
    own_tokens, d_output = tokens[0], cotangent[0]
    gain_row_one, gain_row_two = gain_one.reshape(1, width), gain_two.reshape(1, width)
    lanes = -(-(experts + 3) // 128) * 128
    logit_weight = jnp.concatenate(
        [router, mix_weight, jnp.zeros((width, lanes - experts - 2), BF16)], axis=1
    )

    first = normalize(own_tokens.astype(F32), gain_one.astype(F32))[0].astype(BF16)
    first_pieces = gather_pieces(first)
    qkv = to_heads(ids, first_pieces, w_qkv)
    attended_part = attend(seg_row, seg_col, qkv)
    attended = lax.all_to_all(
        attended_part.reshape(narrow, rows, part), "narrow", split_axis=0, concat_axis=0, tiled=True
    )
    mid, second, d_dense, slots, d_slots, to_slot, gates = middle(
        attended, w_out, own_tokens, d_output, gain_row_two, logit_weight, routes, experts, capacity
    )

    def to_experts(values):
        values = values.reshape(experts, capacity, width)
        arrived = lax.all_to_all(values, "wide", split_axis=0, concat_axis=0, tiled=True)
        return arrived.reshape(experts * capacity, width)

    def to_tokens(both):
        both = both.reshape(experts, capacity, width)
        back = lax.all_to_all(both, "wide", split_axis=0, concat_axis=0, tiled=True)
        return back.reshape(experts * capacity, width)

    expert_rows = to_experts(slots)

    slot = units // (wide * narrow)
    dense_units = units // narrow
    dense_block = min(512, dense_units)
    if slot % 128 == 0:
        slices = dense_block // slot
        dense_places = [
            (lambda f, s, i=i: (f * slices + i) * narrow + s[0]) for i in range(slices)
        ]
        fc1_part, fc2_part = w_fc1, w_fc2
    else:
        dense_places = [lambda f, s: f]
        fc1_part = lax.dynamic_index_in_dim(
            w_fc1.reshape(width, wide, narrow, slot), own, 2, keepdims=False
        ).reshape(width, dense_units)
        fc2_part = lax.dynamic_index_in_dim(
            w_fc2.reshape(wide, narrow, slot, width), own, 1, keepdims=False
        ).reshape(dense_units, width)
    second_pieces = gather_pieces(second)
    d_dense_pieces = gather_pieces(d_dense)
    dense_hidden, dense_slope, dense_mine, dense_other = feed(
        forward_kernel, "dense_forward", ids, second_pieces, fc1_part, fc2_part,
        dense_units, dense_places, dense_block,
    )
    expert_rows = tied(expert_rows, dense_hidden)
    expert_d_rows = to_experts(tied(d_slots, expert_rows))
    expert_rows = [expert_rows, swap(expert_rows, "narrow", 1)]
    expert_d_rows = [expert_d_rows, swap(expert_d_rows, "narrow", 1)]
    dense_sums = scatter_addends(dense_mine, dense_other, rows)
    d_dense_pre, d_second_mine, d_second_other = feed(
        backward_kernel, "dense_backward", ids, d_dense_pieces, fc1_part, fc2_part,
        dense_units, dense_places, dense_block, dense_slope,
    )
    d_second_sums = scatter_addends(d_second_mine, d_second_other, rows)

    quarter = units // narrow
    expert_block = min(512, quarter)
    per_quarter = quarter // expert_block
    expert_places = [
        lambda f, s: (2 * (f // per_quarter) + s[1]) * per_quarter + f % per_quarter
    ]
    expert_rows = [tied(expert_rows[0], d_second_mine), expert_rows[1]]
    expert_hidden, expert_slope, produced_mine, produced_other = feed(
        forward_kernel, "expert_forward", ids, expert_rows, expert_in[0], expert_out[0],
        units // 2, expert_places, expert_block,
    )
    produced = add_to_bf16(produced_mine, swap(produced_other, "narrow", 1))
    back = to_tokens(produced)
    out_gone = out_leaves(ids, expert_d_rows, expert_hidden) if narrow == 4 else produced
    d_expert_pre, d_sent_mine, d_sent_other = feed(
        backward_kernel, "expert_backward", ids, expert_d_rows, expert_in[0], expert_out[0],
        units // 2, expert_places, expert_block, tied(expert_slope, out_gone, produced, dense_sums[-1], d_second_sums[-1]),
    )
    d_back = to_tokens(add_to_bf16(d_sent_mine, swap(d_sent_other, "narrow", 1)))
    dense_hidden = tied(dense_hidden, back, d_expert_pre)
    if slot % 128 == 0:
        feed_keep, feed_gone = feed_grads(
            ids, second_pieces, d_dense_pieces, dense_hidden, d_dense_pre
        )
    else:
        fc1_sum = wide_sum(
            grad("fc1_grad", ids, second_pieces, [d_dense_pre], 256, width // 256, lambda i, s: i)
        )
        fc2_sum = wide_sum(
            grad("fc2_grad", ids, [dense_hidden], d_dense_pieces, 256, dense_units // 256,
                 lambda i, s: i)
        )

    in_gone = in_leaves(ids, expert_rows, d_expert_pre) if narrow == 4 else d_back
    out_came, in_came = swap(out_gone, "narrow", 2), swap(in_gone, "narrow", 2)

    output, d_mid, d_attn, d_attended, small = merge(
        back, d_back, tied(to_slot, in_gone, out_came), gates, routes, mid, second, d_output, gain_row_two, logit_weight,
        w_out, dense_sums, d_second_sums, experts, narrow,
    )
    d_attended_part = lax.all_to_all(
        d_attended, "narrow", split_axis=0, concat_axis=0, tiled=True
    ).reshape(length, part)
    out_mine, out_other = out_grad(ids, attended, d_attn)
    out_sum = scatter_columns(out_mine, out_other, part)
    if slot % 128 == 0:
        feed_sum = lax.psum_scatter(
            add_to_bf16(tied(feed_keep, d_attended), swap(feed_gone, "wide", 1)),
            "wide",
            scatter_dimension=0,
            axis_index_groups=[[2 * z + y for z in range(wide // 2)] for y in range(2)],
            tiled=True,
        )
    d_qkv = attend_back(seg_row, seg_col, tied(qkv, out_mine), d_attended_part)
    d_first_mine, d_first_other = from_heads(ids, d_qkv, w_qkv)
    d_first_sums = scatter_addends(d_first_mine, d_first_other, rows)
    heads_sum = wide_sum_at_once(
        heads_grad(ids, first_pieces, tied(d_qkv, in_came), out_sum, small)
    )
    input_grad = finish(own_tokens, gain_row_one, d_mid, d_first_sums)
    grad_expert_in, grad_expert_out = expert_grads(
        ids, expert_rows, expert_d_rows, expert_hidden, d_expert_pre, own, out_came, in_came, d_qkv
    )

    held = width // wide
    if slot % 128 == 0:
        grad_fc1, grad_fc2 = put_feed(narrow_all(feed_sum), width)
    else:
        fc1_all, fc2_all = narrow_all(fc1_sum), narrow_all(fc2_sum)
        grad_fc1 = (
            fc1_all.reshape(narrow, held, wide, slot).transpose(1, 2, 0, 3).reshape(held, units)
        ).astype(F32)
        grad_fc2 = fc2_all.reshape(units // wide, width).astype(F32)
    grad_qkv, grad_out, grad_router, grad_mix, grad_gain_one, grad_gain_two = put_heads(
        ids, gather_pieces(heads_sum), w_qkv, gain_one, experts
    )
    return (
        output[None],
        input_grad[None],
        grad_qkv,
        grad_out,
        grad_fc1,
        grad_fc2,
        grad_router,
        grad_mix,
        grad_gain_one.reshape(held),
        grad_gain_two.reshape(held),
        grad_expert_in[None],
        grad_expert_out[None],
    )


def solution(mesh):
    return jax.shard_map(
        per_device,
        mesh=mesh,
        in_specs=(
            P("wide", "narrow", None),
            P("wide", None),
            P(("narrow", "wide"), None),
            P(),
            P(),
            P(),
            P(),
            P(),
            P(),
            P(),
            P(),
            P("wide", None, None),
            P("wide", None, None),
            P("wide", "narrow", None),
        ),
        out_specs=(
            P("wide", "narrow", None),
            P("wide", "narrow", None),
            P("wide", None),
            P("wide", None),
            P("wide", None),
            P("wide", None),
            P("wide", None),
            P("wide", None),
            P("wide"),
            P("wide"),
            P("wide", "narrow", None),
            P("wide", "narrow", None),
        ),
        check_vma=False,
    )
```

time: 1560 us -> 423 us (0.27)
  waiting for transfers between devices: 1200 us -> 133 us
  matrix products: 176 us -> 0 us
  Pallas kernels: 0 us -> 171 us
  other arithmetic: 61.6 us -> 25.3 us
  blocking collectives: 25.8 us -> 0 us
  starting transfers between devices: 28.5 us -> 53.4 us
  local copies, waits for them, and re-layouts: 37.4 us -> 17.1 us
    reduce_scatter x8 -> x1, waiting for transfers between devices: 1010 us -> 0.02 us  [per_device(): lax.psum_scatter(add_to_bf16(tied(feed_keep, d_attended), swap(feed_gone,...]
    dot_general x29 -> x0, matrix products: 175 us -> none  [the longest x5 32.4 us: across(): lax.dot_general(left, right, (((0,), (0,)), ((), ())), preferred_element_...]
    pallas_call x0 -> x22, Pallas kernels: none -> 171 us  [the longest x4 53.5 us: feed(): pl.pallas_call(functools.partial(kernel, len(pieces), len(places)), grid_...]
    psum x1 -> x0, waiting for transfers between devices: 68.2 us -> none  [per_device(): lax.psum(part_qkv.astype(jnp.bfloat16), 'narrow').astype(jnp.float32)]
    unnamed x12 -> x2, waiting for transfers between devices: 61.5 us -> 0.69 us
    ppermute x0 -> x28, waiting for transfers between devices: none -> 60 us  [swap(): return lax.ppermute(values, axis, [(i, i ^ bit) for i in range(size)])]
    all_to_all x4 -> x7, waiting for transfers between devices: 29.8 us -> 72 us  [the longest x1 40.8 us: wide_sum_at_once(): lax.all_to_all(blocks, 'wide', split_axis=0, concat_axis=0, tiled=True)]
    all_gather x1, waiting for transfers between devices: 34.7 us -> 0.01 us  [narrow_all(): return lax.all_gather(values, 'narrow', axis=0, tiled=False)]
  transfers between devices with their start and end apart: 15 -> 37, of which waited for: 14 -> 12; matrix products, arithmetic and copies ran while one was open for 10% -> 7% of each run, Pallas kernels for 0% -> 35%
where the time goes in v1:
time: 423 us; the launch traced here: 414 us
  Pallas kernels  171 us (40%)
  waiting for transfers between devices  133 us (31%)
  starting transfers between devices  53.4 us (13%)
  other arithmetic  25.3 us (6%)
  local copies, waits for them, and re-layouts  17.1 us (4%)
  between operations  14.8 us (3%)
    ppermute x28, waiting for transfers between devices, swap(): return lax.ppermute(values, axis, [(i, i ^ bit) for i in range(size)])  60 us
    pallas_call x4, Pallas kernels, feed(): pl.pallas_call(functools.partial(kernel, len(pieces), len(places)), grid_...  53.5 us
    all_to_all x1, waiting for transfers between devices, wide_sum_at_once(): lax.all_to_all(blocks, 'wide', split_axis=0, concat_axis=0, tiled=True)  40.8 us
    pallas_call x5, Pallas kernels, grad(): pl.pallas_call(functools.partial(grad_kernel, len(lefts), len(rights)), g...  30.3 us
    all_to_all x2, waiting for transfers between devices, to_tokens(): back = lax.all_to_all(both, 'wide', split_axis=0, concat_axis=0, tiled=True)  21.4 us
    convert_element_type x8, other arithmetic, add_to_bf16(): return (left.astype(F32) + right.astype(F32)).astype(BF16)  18.1 us
    ppermute x28, starting transfers between devices, swap(): return lax.ppermute(values, axis, [(i, i ^ bit) for i in range(size)])  16.6 us
    pallas_call x1, Pallas kernels, attend_back(): pl.pallas_call(functools.partial(attend_back_kernel, lax.axis_size('narro...  14.9 us
  transfers between devices with their start and end apart: 37, of which 12 were waited for; matrix products, arithmetic and copies ran while one was open for 7% of the time, Pallas kernels for 35%

profile of v1, /device:TPU:0, one launch (start us, length us, event | category | flops | bytes accessed | tf_op | source)
XLA Modules:
  0.0 414.3 jit_solution(8019099946649522446)
XLA Ops:
  14.8 11.9 %collective-permute-done.refs_1_ = bf16[256,1024]{1,0:T(8,128)(2,1)S(1)} collective-permute-done((bf16[256,1024]{1,0:T(8,128)(2,1)S(1)}, bf16[256,1024]{1,0:T(8,128)(2,1)S(1)}, u32[]{:S(2)}, u32[]{:S(2)}) %collective-permute-start) | collective-permute-done | bytes 524320 | tf_op jit(solution)/shard_map/ppermute | solution.py:55
  30.0 5.9 %to_heads.1.qkv_ref = bf16[1024,768]{1,0:T(8,128)(2,1)} custom-call(s32[4]{0:T(128)} %pad_add_fusion.ids_ref, bf16[256,1024]{1,0:T(8,128)(2,1)} %copy-done.4, bf16[256,1024]{1,0:T(8,128)(2,1)} %copy-done.13, bf16[256,1024]{1,0:T(8,128)(2,1)} %copy-done.14, bf16[256,1024]{1,0:T(8,128)(2,1)} %copy-done.15, bf16[1024,3072]{1,0:T(8,128)(2,1)} %refs_4_.7), custom_call_target="tpu_custom_call" | custom-call | flops 1610612736 | bytes 3670016 | tf_op jit(solution)/shard_map/to_heads/pallas_call | solution.py:132
  35.9 11.7 %attend.1 = bf16[1024,256]{1,0:T(8,128)(2,1)} custom-call(s32[1,1024]{1,0:T(1,128)} %seg_row_ref.3, s32[1024,1]{1,0:T(8,128)} %copy.33.seg_col_ref, bf16[1024,768]{1,0:T(8,128)(2,1)} %to_heads.1.qkv_ref), custom_call_target="tpu_custom_call" | custom-call | flops 1073741824 | bytes 4194304 | tf_op jit(solution)/shard_map/attend/pallas_call | solution.py:265
  54.1 6.1 %all-to-all-done.parts_ref.attended_ref = bf16[4,256,256]{2,1,0:T(8,128)(2,1)S(1)} async-done(((bf16[4,256,256]{2,1,0:T(8,128)(2,1)}), bf16[4,256,256]{2,1,0:T(8,128)(2,1)S(1)}, u32[]{:S(2)}, u32[]{:S(2)}) %all-to-all-start) | async-done | bytes 524320 | tf_op jit(solution)/shard_map/all_to_all | solution.py:979
  61.1 6.0 %middle.1 = (f32[256,1024]{1,0:T(8,128)}, bf16[256,1024]{1,0:T(8,128)(2,1)}, bf16[256,1024]{1,0:T(8,128)(2,1)}, bf16[512,1024]{1,0:T(8,128)(2,1)}, bf16[512,1024...) custom-call(bf16[4,256,256]{2,1,0:T(8,128)(2,1)} %copy-done.12, bf16[1024,1024]{1,0:T(8,128)(2,1)} %w_out_ref.3, ...), custom_call_target="tpu_custom_call" | custom-call | flops 1073741824 | bytes 6291456 | tf_op jit(solution)/shard_map/middle/pallas_call | solution.py:360
  67.1 6.1 %all-to-all-start.1 = ((bf16[8,64,1024]{2,1,0:T(8,128)(2,1)}), bf16[8,64,1024]{2,1,0:T(8,128)(2,1)S(1)}, u32[]{:S(2)}, u32[]{:S(2)}) async-start(bf16[8,64,1024]{2,1,0:T(8,128)(2,1)} %bitcast.51), calls=%async_computation.1 | async-start | bytes 2097152 | tf_op jit(solution)/shard_map/all_to_all | solution.py:988
  73.7 12.8 %collective-permute-done.3.refs_1_ = bf16[256,1024]{1,0:T(8,128)(2,1)S(1)} collective-permute-done((bf16[256,1024]{1,0:T(8,128)(2,1)S(1)}, bf16[256,1024]{1,0:T(8,128)(2,1)S(1)}, u32[]{:S(2)}, u32[]{:S(2)}) %collective-permute-start.3) | collective-permute-done | bytes 524320 | tf_op jit(solution)/shard_map/ppermute | solution.py:55
  89.2 11.0 %dense_forward.1 = (bf16[1024,1024]{1,0:T(8,128)(2,1)}, bf16[1024,1024]{1,0:T(8,128)(2,1)}, bf16[512,1024]{1,0:T(8,128)(2,1)}, bf16[512,1024]{1,0:T(8,128)(2,1)}) custom-call(s32[4]{0:T(128)} %pad_add_fusion.ids_ref, bf16[256,1024]{1,0:T(8,128)(2,1)} %get-tuple-element.63.refs_0_.second_ref, bf16[256,1024]{1,0:T(8,128)(2,1)} %copy-done.19, ...), custom_call_target="tpu_custom_call" | custom-call | flops 4294967296 | bytes 12582912 | tf_op jit(solution)/shard_map/dense_forward/pallas_call | solution.py:589
  101.1 6.2 %all-to-all-start.3 = ((bf16[8,64,1024]{2,1,0:T(8,128)(2,1)}), bf16[8,64,1024]{2,1,0:T(8,128)(2,1)S(1)}, u32[]{:S(2)}, u32[]{:S(2)}) async-start(bf16[8,64,1024]{2,1,0:T(8,128)(2,1)} %bitcast.50), calls=%async_computation.3 | async-start | bytes 2097152 | tf_op jit(solution)/shard_map/all_to_all | solution.py:988
  107.6 10.7 %dense_backward.1 = (bf16[1024,1024]{1,0:T(8,128)(2,1)}, bf16[512,1024]{1,0:T(8,128)(2,1)}, bf16[512,1024]{1,0:T(8,128)(2,1)}) custom-call(s32[4]{0:T(128)} %pad_add_fusion.ids_ref, bf16[256,1024]{1,0:T(8,128)(2,1)} %get-tuple-element.66.refs_0_.refs_4_, bf16[256,1024]{1,0:T(8,128)(2,1)} %collective-permute-done.6.refs_1_.refs_5_, ...), custom_call_target="tpu_custom_call" | custom-call | flops 4294967296 | bytes 12582912 | tf_op jit(solution)/shard_map/dense_backward/pallas_call | solution.py:589
  119.6 16.3 %expert_forward.1 = (bf16[1024,2048]{1,0:T(8,128)(2,1)}, bf16[1024,2048]{1,0:T(8,128)(2,1)}, bf16[512,1024]{1,0:T(8,128)(2,1)}, bf16[512,1024]{1,0:T(8,128)(2,1)}) custom-call(s32[4]{0:T(128)} %pad_add_fusion.ids_ref, bf16[512,1024]{1,0:T(8,128)(2,1)} %bitcast.32, bf16[512,1024]{1,0:T(8,128)(2,1)} %copy-done.1, bf16[1024,4096]{1,0:T(8,128)(2,1)} %bitcast.56, ...), custom_call_target="tpu_custom_call" | custom-call | flops 8589934592 | bytes 20971520 | tf_op jit(solution)/shard_map/expert_forward/pallas_call | solution.py:589
  145.9 6.0 %all-to-all-start.2 = ((bf16[8,64,1024]{2,1,0:T(8,128)(2,1)}), bf16[8,64,1024]{2,1,0:T(8,128)(2,1)S(1)}, u32[]{:S(2)}, u32[]{:S(2)}) async-start(bf16[8,64,1024]{2,1,0:T(8,128)(2,1)} %bitcast.12), calls=%async_computation.2 | async-start | bytes 2097152 | tf_op jit(solution)/shard_map/all_to_all | solution.py:993
  152.9 6.1 %out_gone.1 = bf16[1024,1024]{1,0:T(8,128)(2,1)} custom-call(s32[4]{0:T(128)} %pad_add_fusion.ids_ref, bf16[1024,2048]{1,0:T(8,128)(2,1)} %get-tuple-element.111.refs_0_, bf16[512,1024]{1,0:T(8,128)(2,1)} %bitcast.40, bf16[512,1024]{1,0:T(8,128)(2,1)} %copy-done.5), custom_call_target="tpu_custom_call" | custom-call | flops 2147483648 | bytes 8388608 | tf_op jit(solution)/shard_map/out_gone/pallas_call | solution.py:633
  159.1 5.7 %collective-permute-done.15.refs_5_ = bf16[256,1024]{1,0:T(8,128)(2,1)} collective-permute-done((bf16[256,1024]{1,0:T(8,128)(2,1)}, bf16[256,1024]{1,0:T(8,128)(2,1)}, u32[]{:S(2)}, u32[]{:S(2)}) %collective-permute-start.15) | collective-permute-done | bytes 524320 | tf_op jit(solution)/shard_map/ppermute | solution.py:55
  164.7 15.5 %expert_backward.1 = (bf16[1024,2048]{1,0:T(8,128)(2,1)}, bf16[512,1024]{1,0:T(8,128)(2,1)}, bf16[512,1024]{1,0:T(8,128)(2,1)}) custom-call(s32[4]{0:T(128)} %pad_add_fusion.ids_ref, bf16[512,1024]{1,0:T(8,128)(2,1)} %bitcast.41, bf16[512,1024]{1,0:T(8,128)(2,1)} %copy-done.5, bf16[1024,4096]{1,0:T(8,128)(2,1)} %bitcast.57, bf16[4096,1024]{1,0:T(8,128)(2,1)} %bitcast.59, ...), custom_call_target="tpu_custom_call" | custom-call | flops 8589934592 | bytes 20971520 | tf_op jit(solution)/shard_map/expert_backward/pallas_call | solution.py:589
  181.0 10.0 %feed_grads.1 = (bf16[512,2048]{1,0:T(8,128)(2,1)}, bf16[512,2048]{1,0:T(8,128)(2,1)}) custom-call(s32[4]{0:T(128)} %pad_add_fusion.ids_ref, bf16[1024,1024]{1,0:T(8,128)(2,1)} %get-tuple-element.100.hidden_ref, bf16[1024,1024]{1,0:T(8,128)(2,1)} %get-tuple-element.101.d_pre_ref, bf16[256,1024]{1,0:T(8,128)(2,1)} %get-tuple-element.63.refs_0_.second_ref, ...), custom_call_target="tpu_custom_call" | custom-call | flops 4294967296 | bytes 12582912 | tf_op jit(solution)/shard_map/feed_grads/pallas_call | solution.py:673
  194.4 4.5 %all-to-all-start.4 = ((bf16[8,64,1024]{2,1,0:T(8,128)(2,1)}), bf16[8,64,1024]{2,1,0:T(8,128)(2,1)S(1)}, u32[]{:S(2)}, u32[]{:S(2)}) async-start(bf16[8,64,1024]{2,1,0:T(8,128)(2,1)} %bitcast.16), calls=%async_computation.4 | async-start | bytes 2097152 | tf_op jit(solution)/shard_map/all_to_all | solution.py:993
  199.0 6.6 %in_gone.1 = bf16[512,2048]{1,0:T(8,128)(2,1)} custom-call(s32[4]{0:T(128)} %pad_add_fusion.ids_ref, bf16[512,1024]{1,0:T(8,128)(2,1)} %bitcast.33, bf16[512,1024]{1,0:T(8,128)(2,1)} %copy-done.1, bf16[1024,2048]{1,0:T(8,128)(2,1)} %get-tuple-element.83.refs_2_), custom_call_target="tpu_custom_call" | custom-call | flops 2147483648 | bytes 9437184 | tf_op jit(solution)/shard_map/in_gone/pallas_call | solution.py:633
  206.8 22.2 %collective-permute-done.17.refs_3_ = bf16[1024,1024]{1,0:T(8,128)(2,1)} collective-permute-done((bf16[1024,1024]{1,0:T(8,128)(2,1)}, bf16[1024,1024]{1,0:T(8,128)(2,1)}, u32[]{:S(2)}, u32[]{:S(2)}) %collective-permute-start.17) | collective-permute-done | bytes 2097184 | tf_op jit(solution)/shard_map/ppermute | solution.py:55
  229.0 21.4 %all-to-all-done.4 = bf16[8,64,1024]{2,1,0:T(8,128)(2,1)S(1)} async-done(((bf16[8,64,1024]{2,1,0:T(8,128)(2,1)}), bf16[8,64,1024]{2,1,0:T(8,128)(2,1)S(1)}, u32[]{:S(2)}, u32[]{:S(2)}) %all-to-all-start.4) | async-done | bytes 1048608 | tf_op jit(solution)/shard_map/all_to_all | solution.py:993
  251.4 7.5 %merge.1 = (bf16[256,1024]{1,0:T(8,128)(2,1)}, f32[256,1024]{1,0:T(8,128)}, bf16[4,256,256]{2,1,0:T(8,128)(2,1)}, bf16[4,256,256]{2,1,0:T(8,128)(2,1)}, bf16[1024,128]{1,0:T(8,128)(2,1)}) custom-call(bf16[512,1024]{1,0:T(8,128)(2,1)} %bitcast.45, bf16[512,1024]{1,0:T(8,128)(2,1)} %bitcast.46, bf16[256,512]{1,0:T(8,128)(2,1)} %get-tuple-element.84.to_slot_ref, ...), custom_call_target="tpu_custom_call" | custom-call | flops 1073741824 | bytes 10485760 | tf_op jit(solution)/shard_map/merge/pallas_call | solution.py:450
  262.8 4.8 %out_grad.1 = (bf16[1024,512]{1,0:T(8,128)(2,1)}, bf16[1024,512]{1,0:T(8,128)(2,1)}) custom-call(s32[4]{0:T(128)} %pad_add_fusion.ids_ref, bf16[4,256,256]{2,1,0:T(8,128)(2,1)} %copy-done.12, bf16[4,256,256]{2,1,0:T(8,128)(2,1)} %get-tuple-element.89.d_ref), custom_call_target="tpu_custom_call" | custom-call | flops 536870912 | bytes 8388608 | tf_op jit(solution)/shard_map/out_grad/pallas_call | solution.py:741
  267.6 4.4 %all-to-all-start.5 = ((bf16[4,256,256]{2,1,0:T(8,128)(2,1)}), bf16[4,256,256]{2,1,0:T(8,128)(2,1)}, u32[]{:S(2)}, u32[]{:S(2)}) async-start(bf16[4,256,256]{2,1,0:T(8,128)(2,1)} %get-tuple-element.92), calls=%async_computation.5 | async-start | bytes 1048576 | tf_op jit(solution)/shard_map/all_to_all | solution.py:1072
  281.2 14.9 %attend_back.1.d_ref.refs_4_ = bf16[1024,768]{1,0:T(8,128)(2,1)} custom-call(s32[1,1024]{1,0:T(1,128)} %seg_row_ref.3, s32[1024,1]{1,0:T(8,128)} %copy.33.seg_col_ref, bf16[1024,768]{1,0:T(8,128)(2,1)} %to_heads.1.qkv_ref, bf16[1024,256]{1,0:T(8,128)(2,1)} %bitcast.19.d_ref), custom_call_target="tpu_custom_call" | custom-call | flops 2684354560 | bytes 4194304 | tf_op jit(solution)/shard_map/attend_back/pallas_call | solution.py:278
  298.7 6.7 %heads_grad.1 = bf16[1024,1152]{1,0:T(8,128)(2,1)} custom-call(s32[4]{0:T(128)} %pad_add_fusion.ids_ref, bf16[256,1024]{1,0:T(8,128)(2,1)} %copy-done.4, bf16[256,1024]{1,0:T(8,128)(2,1)} %copy-done.13, bf16[256,1024]{1,0:T(8,128)(2,1)} %copy-done.14, bf16[256,1024]{1,0:T(8,128)(2,1)} %copy-done.15, bf16[1024,768]{1,0:T(8,128)(2,1)} %attend_back.1.d_ref.refs_4_, ...), custom_call_target="tpu_custom_call" | custom-call | flops 1610612736 | bytes 4194304 | tf_op jit(solution)/shard_map/heads_grad/pallas_call | solution.py:707
  305.4 5.8 %all-to-all-start.6 = ((bf16[8,128,1152]{2,1,0:T(8,128)(2,1)}), bf16[8,128,1152]{2,1,0:T(8,128)(2,1)S(1)}, u32[]{:S(2)}, u32[]{:S(2)}) async-start(bf16[8,128,1152]{2,1,0:T(8,128)(2,1)} %bitcast.43), calls=%async_computation.6 | async-start | bytes 4718592 | tf_op jit(solution)/shard_map/all_to_all | solution.py:878
  311.9 5.3 %from_heads.1 = (bf16[512,1024]{1,0:T(8,128)(2,1)}, bf16[512,1024]{1,0:T(8,128)(2,1)}) custom-call(s32[4]{0:T(128)} %pad_add_fusion.ids_ref, bf16[1024,768]{1,0:T(8,128)(2,1)} %attend_back.1.d_ref.refs_4_, bf16[1024,3072]{1,0:T(8,128)(2,1)} %refs_4_.7, bf16[1024,3072]{1,0:T(8,128)(2,1)} %refs_4_.7, bf16[1024,3072]{1,0:T(8,128)(2,1)} %refs_4_.7), custom_call_target="tpu_custom_call" | custom-call | flops 1610612736 | bytes 4194304 | tf_op jit(solution)/shard_map/from_heads/pallas_call | solution.py:165
  317.2 5.7 %in_other.1 = bf16[256,2048]{1,0:T(8,128)(2,1)} custom-call(s32[4]{0:T(128)} %pad_add_fusion.ids_ref, bf16[512,1024]{1,0:T(8,128)(2,1)} %bitcast.34, bf16[512,1024]{1,0:T(8,128)(2,1)} %copy-done.1, bf16[1024,2048]{1,0:T(8,128)(2,1)} %get-tuple-element.83.refs_2_, bf16[512,2048]{1,0:T(8,128)(2,1)} %copy-done.3), custom_call_target="tpu_custom_call" | custom-call | flops 1073741824 | bytes 6815744 | tf_op jit(solution)/shard_map/in_other/pallas_call | solution.py:633
  323.5 40.8 %all-to-all-done.6 = bf16[8,128,1152]{2,1,0:T(8,128)(2,1)S(1)} async-done(((bf16[8,128,1152]{2,1,0:T(8,128)(2,1)}), bf16[8,128,1152]{2,1,0:T(8,128)(2,1)S(1)}, u32[]{:S(2)}, u32[]{:S(2)}) %all-to-all-start.6) | async-done | bytes 2359328 | tf_op jit(solution)/shard_map/all_to_all | solution.py:878
  369.9 5.6 %collective-permute-done.23.refs_1_ = bf16[128,1152]{1,0:T(8,128)(2,1)S(1)} collective-permute-done((bf16[128,1152]{1,0:T(8,128)(2,1)}, bf16[128,1152]{1,0:T(8,128)(2,1)S(1)}, u32[]{:S(2)}, u32[]{:S(2)}) %collective-permute-start.23) | collective-permute-done | bytes 294944 | tf_op jit(solution)/shard_map/ppermute | solution.py:55
  375.5 5.0 %in_kept.1.whole_ref = f32[256,4096]{1,0:T(8,128)} custom-call(s32[4]{0:T(128)} %pad_add_fusion.ids_ref, bf16[512,1024]{1,0:T(8,128)(2,1)} %bitcast.35, bf16[512,1024]{1,0:T(8,128)(2,1)} %copy-done.1, bf16[1024,2048]{1,0:T(8,128)(2,1)} %get-tuple-element.83.refs_2_, bf16[512,2048]{1,0:T(8,128)(2,1)} %copy-done.3), custom_call_target="tpu_custom_call" | custom-call | flops 1073741824 | bytes 5242880 | tf_op jit(solution)/shard_map/in_kept/pallas_call | solution.py:633
  383.7 6.8 %out_kept.1 = f32[1024,1024]{1,0:T(8,128)} custom-call(s32[4]{0:T(128)} %pad_add_fusion.ids_ref, bf16[1024,2048]{1,0:T(8,128)(2,1)} %get-tuple-element.111.refs_0_, bf16[512,1024]{1,0:T(8,128)(2,1)} %bitcast.42, bf16[512,1024]{1,0:T(8,128)(2,1)} %copy-done.5, bf16[1024,1024]{1,0:T(8,128)(2,1)} %collective-permute-done.17.refs_3_), custom_call_target="tpu_custom_call" | custom-call | flops 2147483648 | bytes 8388608 | tf_op jit(solution)/shard_map/out_kept/pallas_call | solution.py:633
  (159 shorter events, 83.4 us)
Async XLA Ops:
  11.8 14.9 %collective-permute-start = (bf16[256,1024]{1,0:T(8,128)(2,1)S(1)}, bf16[256,1024]{1,0:T(8,128)(2,1)S(1)}, u32[]{:S(2)}, u32[]{:S(2)}) collective-permute-start(bf16[256,1024]{1,0:T(8,128)(2,1)S(1)} %fusion.4.refs_0_), channel_id=1, source_target_pairs={{0,16},{8,24},{16,0},{24,8},{1,17},{9,25},{17,1},{25,9},{2,18},{10... | collective-permute-start | bytes 1572872 | tf_op jit(solution)/shard_map/ppermute | solution.py:55
  14.8 13.6 %collective-permute-start.1 = (bf16[256,1024]{1,0:T(8,128)(2,1)S(1)}, bf16[256,1024]{1,0:T(8,128)(2,1)S(1)}, u32[]{:S(2)}, u32[]{:S(2)}) collective-permute-start(bf16[256,1024]{1,0:T(8,128)(2,1)S(1)} %fusion.4.refs_0_), channel_id=1, source_target_pairs={{0,8},{8,0},{16,24},{24,16},{1,9},{9,1},{17,25},{25,17},{2,10},{10... | collective-permute-start | bytes 1572872 | tf_op jit(solution)/shard_map/ppermute | solution.py:55
  47.6 12.7 %all-to-all-start = ((bf16[4,256,256]{2,1,0:T(8,128)(2,1)}), bf16[4,256,256]{2,1,0:T(8,128)(2,1)S(1)}, u32[]{:S(2)}, u32[]{:S(2)}) async-start(bf16[4,256,256]{2,1,0:T(8,128)(2,1)} %bitcast.53), calls=%async_computation | async-start | bytes 1048576 | tf_op jit(solution)/shard_map/all_to_all | solution.py:979
  67.1 33.1 %all-to-all-start.1 = ((bf16[8,64,1024]{2,1,0:T(8,128)(2,1)}), bf16[8,64,1024]{2,1,0:T(8,128)(2,1)S(1)}, u32[]{:S(2)}, u32[]{:S(2)}) async-start(bf16[8,64,1024]{2,1,0:T(8,128)(2,1)} %bitcast.51), calls=%async_computation.1 | async-start | bytes 2097152 | tf_op jit(solution)/shard_map/all_to_all | solution.py:988
  73.2 13.2 %collective-permute-start.3 = (bf16[256,1024]{1,0:T(8,128)(2,1)S(1)}, bf16[256,1024]{1,0:T(8,128)(2,1)S(1)}, u32[]{:S(2)}, u32[]{:S(2)}) collective-permute-start(bf16[256,1024]{1,0:T(8,128)(2,1)S(1)} %copy-done.10), channel_id=1, source_target_pairs={{0,16},{8,24},{16,0},{24,8},{1,17},{9,25},{17,1},{25,9},{2,18},{10... | collective-permute-start | bytes 1572872 | tf_op jit(solution)/shard_map/ppermute | solution.py:55
  73.7 13.5 %collective-permute-start.4 = (bf16[256,1024]{1,0:T(8,128)(2,1)S(1)}, bf16[256,1024]{1,0:T(8,128)(2,1)S(1)}, u32[]{:S(2)}, u32[]{:S(2)}) collective-permute-start(bf16[256,1024]{1,0:T(8,128)(2,1)S(1)} %copy-done.10), channel_id=1, source_target_pairs={{0,8},{8,0},{16,24},{24,16},{1,9},{9,1},{17,25},{25,17},{2,10},{10... | collective-permute-start | bytes 1572872 | tf_op jit(solution)/shard_map/ppermute | solution.py:55
  86.5 14.7 %collective-permute-start.6 = (bf16[256,1024]{1,0:T(8,128)(2,1)}, bf16[256,1024]{1,0:T(8,128)(2,1)}, u32[]{:S(2)}, u32[]{:S(2)}) collective-permute-start(bf16[256,1024]{1,0:T(8,128)(2,1)} %get-tuple-element.66.refs_0_.refs_4_), channel_id=1, source_target_pairs={{0,16},{8,24},{16,0},{24,8},{1,17},{9,25},{17,1},{25,9},{2,18},{10... | collective-permute-start | bytes 1572872 | tf_op jit(solution)/shard_map/ppermute | solution.py:55
  100.3 18.4 %collective-permute-start.9 = (bf16[512,1024]{1,0:T(8,128)(2,1)S(1)}, bf16[512,1024]{1,0:T(8,128)(2,1)S(1)}, u32[]{:S(2)}, u32[]{:S(2)}) collective-permute-start(bf16[512,1024]{1,0:T(8,128)(2,1)S(1)} %bitcast.31), channel_id=1, source_target_pairs={{0,8},{8,0},{16,24},{24,16},{1,9},{9,1},{17,25},{25,17},{2,10},{10... | collective-permute-start | bytes 3145736 | tf_op jit(solution)/shard_map/ppermute | solution.py:55
  101.1 35.2 %all-to-all-start.3 = ((bf16[8,64,1024]{2,1,0:T(8,128)(2,1)}), bf16[8,64,1024]{2,1,0:T(8,128)(2,1)S(1)}, u32[]{:S(2)}, u32[]{:S(2)}) async-start(bf16[8,64,1024]{2,1,0:T(8,128)(2,1)} %bitcast.50), calls=%async_computation.3 | async-start | bytes 2097152 | tf_op jit(solution)/shard_map/all_to_all | solution.py:988
  107.3 29.2 %collective-permute-start.12 = (bf16[512,1024]{1,0:T(8,128)(2,1)}, bf16[512,1024]{1,0:T(8,128)(2,1)}, u32[]{:S(2)}, u32[]{:S(2)}) collective-permute-start(bf16[512,1024]{1,0:T(8,128)(2,1)} %get-tuple-element.77), channel_id=1, source_target_pairs={{0,8},{8,0},{16,24},{24,16},{1,9},{9,1},{17,25},{25,17},{2,10},{10... | collective-permute-start | bytes 3145736 | tf_op jit(solution)/shard_map/ppermute | solution.py:55
  118.3 21.4 %collective-permute-start.14 = (bf16[512,1024]{1,0:T(8,128)(2,1)}, bf16[512,1024]{1,0:T(8,128)(2,1)}, u32[]{:S(2)}, u32[]{:S(2)}) collective-permute-start(bf16[512,1024]{1,0:T(8,128)(2,1)} %get-tuple-element.78), channel_id=1, source_target_pairs={{0,8},{8,0},{16,24},{24,16},{1,9},{9,1},{17,25},{25,17},{2,10},{10... | collective-permute-start | bytes 3145736 | tf_op jit(solution)/shard_map/ppermute | solution.py:55
  136.0 7.3 %collective-permute-start.10 = (bf16[512,1024]{1,0:T(8,128)(2,1)}, bf16[512,1024]{1,0:T(8,128)(2,1)}, u32[]{:S(2)}, u32[]{:S(2)}) collective-permute-start(bf16[512,1024]{1,0:T(8,128)(2,1)} %get-tuple-element.71), channel_id=1, source_target_pairs={{0,8},{8,0},{16,24},{24,16},{1,9},{9,1},{17,25},{25,17},{2,10},{10... | collective-permute-start | bytes 3145736 | tf_op jit(solution)/shard_map/ppermute | solution.py:55
  136.3 15.7 %collective-permute-start.11 = (bf16[512,1024]{1,0:T(8,128)(2,1)S(1)}, bf16[512,1024]{1,0:T(8,128)(2,1)S(1)}, u32[]{:S(2)}, u32[]{:S(2)}) collective-permute-start(bf16[512,1024]{1,0:T(8,128)(2,1)S(1)} %bitcast.39), channel_id=1, source_target_pairs={{0,8},{8,0},{16,24},{24,16},{1,9},{9,1},{17,25},{25,17},{2,10},{10... | collective-permute-start | bytes 3145736 | tf_op jit(solution)/shard_map/ppermute | solution.py:55
  139.1 20.0 %collective-permute-start.13 = (bf16[256,1024]{1,0:T(8,128)(2,1)}, bf16[256,1024]{1,0:T(8,128)(2,1)}, u32[]{:S(2)}, u32[]{:S(2)}) collective-permute-start(bf16[256,1024]{1,0:T(8,128)(2,1)} %add_convert_fusion.7), channel_id=1, source_target_pairs={{0,16},{8,24},{16,0},{24,8},{1,17},{9,25},{17,1},{25,9},{2,18},{10... | collective-permute-start | bytes 1572872 | tf_op jit(solution)/shard_map/ppermute | solution.py:55
  142.0 22.8 %collective-permute-start.15 = (bf16[256,1024]{1,0:T(8,128)(2,1)}, bf16[256,1024]{1,0:T(8,128)(2,1)}, u32[]{:S(2)}, u32[]{:S(2)}) collective-permute-start(bf16[256,1024]{1,0:T(8,128)(2,1)} %add_convert_fusion.6), channel_id=1, source_target_pairs={{0,16},{8,24},{16,0},{24,8},{1,17},{9,25},{17,1},{25,9},{2,18},{10... | collective-permute-start | bytes 1572872 | tf_op jit(solution)/shard_map/ppermute | solution.py:55
  145.9 35.0 %all-to-all-start.2 = ((bf16[8,64,1024]{2,1,0:T(8,128)(2,1)}), bf16[8,64,1024]{2,1,0:T(8,128)(2,1)S(1)}, u32[]{:S(2)}, u32[]{:S(2)}) async-start(bf16[8,64,1024]{2,1,0:T(8,128)(2,1)} %bitcast.12), calls=%async_computation.2 | async-start | bytes 2097152 | tf_op jit(solution)/shard_map/all_to_all | solution.py:993
  180.2 12.9 %collective-permute-start.16 = (bf16[512,1024]{1,0:T(8,128)(2,1)}, bf16[512,1024]{1,0:T(8,128)(2,1)S(1)}, u32[]{:S(2)}, u32[]{:S(2)}) collective-permute-start(bf16[512,1024]{1,0:T(8,128)(2,1)} %get-tuple-element.81), channel_id=1, source_target_pairs={{0,8},{8,0},{16,24},{24,16},{1,9},{9,1},{17,25},{25,17},{2,10},{10... | collective-permute-start | bytes 3145736 | tf_op jit(solution)/shard_map/ppermute | solution.py:55
  180.2 48.8 %collective-permute-start.17 = (bf16[1024,1024]{1,0:T(8,128)(2,1)}, bf16[1024,1024]{1,0:T(8,128)(2,1)}, u32[]{:S(2)}, u32[]{:S(2)}) collective-permute-start(bf16[1024,1024]{1,0:T(8,128)(2,1)} %out_gone.1), channel_id=1, source_target_pairs={{0,16},{8,24},{16,0},{24,8},{1,17},{9,25},{17,1},{25,9},{2,18},{10... | collective-permute-start | bytes 6291464 | tf_op jit(solution)/shard_map/ppermute | solution.py:55
  190.9 68.0 %collective-permute-start.26 = (bf16[512,2048]{1,0:T(8,128)(2,1)}, bf16[512,2048]{1,0:T(8,128)(2,1)}, u32[]{:S(2)}, u32[]{:S(2)}) collective-permute-start(bf16[512,2048]{1,0:T(8,128)(2,1)} %get-tuple-element.104), channel_id=1, source_target_pairs={{0,1},{1,0},{2,3},{3,2},{4,5},{5,4},{6,7},{7,6},{8,9},{9,8},{10,11... | collective-permute-start | bytes 6291464 | tf_op jit(solution)/shard_map/ppermute | solution.py:55
  194.4 56.0 %all-to-all-start.4 = ((bf16[8,64,1024]{2,1,0:T(8,128)(2,1)}), bf16[8,64,1024]{2,1,0:T(8,128)(2,1)S(1)}, u32[]{:S(2)}, u32[]{:S(2)}) async-start(bf16[8,64,1024]{2,1,0:T(8,128)(2,1)} %bitcast.16), calls=%async_computation.4 | async-start | bytes 2097152 | tf_op jit(solution)/shard_map/all_to_all | solution.py:993
  199.0 112.2 %reduce-scatter.2.cloned.1.call-start = ((), (), s32[]{:S(2)}) async-start(), calls=%async_computation.8 | async-start | bytes 2621440 | tf_op jit(solution)/shard_map/reduce_scatter | solution.py:1078
  205.6 90.4 %collective-permute-start.20 = (bf16[512,2048]{1,0:T(8,128)(2,1)}, bf16[512,2048]{1,0:T(8,128)(2,1)S(1)}, u32[]{:S(2)}, u32[]{:S(2)}) collective-permute-start(bf16[512,2048]{1,0:T(8,128)(2,1)} %in_gone.1), channel_id=1, source_target_pairs={{0,16},{8,24},{16,0},{24,8},{1,17},{9,25},{17,1},{25,9},{2,18},{10... | collective-permute-start | bytes 6291464 | tf_op jit(solution)/shard_map/ppermute | solution.py:55
  267.6 13.5 %all-to-all-start.5 = ((bf16[4,256,256]{2,1,0:T(8,128)(2,1)}), bf16[4,256,256]{2,1,0:T(8,128)(2,1)}, u32[]{:S(2)}, u32[]{:S(2)}) async-start(bf16[4,256,256]{2,1,0:T(8,128)(2,1)} %get-tuple-element.92), calls=%async_computation.5 | async-start | bytes 1048576 | tf_op jit(solution)/shard_map/all_to_all | solution.py:1072
  275.6 20.5 %collective-permute-start.22 = (bf16[1024,256]{1,0:T(8,128)(2,1)}, bf16[1024,256]{1,0:T(8,128)(2,1)}, u32[]{:S(2)}, u32[]{:S(2)}) collective-permute-start(bf16[1024,256]{1,0:T(8,128)(2,1)} %slice.36), channel_id=1, source_target_pairs={{0,16},{8,24},{16,0},{24,8},{1,17},{9,25},{17,1},{25,9},{2,18},{10... | collective-permute-start | bytes 1572872 | tf_op jit(solution)/shard_map/ppermute | solution.py:55
  305.4 58.9 %all-to-all-start.6 = ((bf16[8,128,1152]{2,1,0:T(8,128)(2,1)}), bf16[8,128,1152]{2,1,0:T(8,128)(2,1)S(1)}, u32[]{:S(2)}, u32[]{:S(2)}) async-start(bf16[8,128,1152]{2,1,0:T(8,128)(2,1)} %bitcast.43), calls=%async_computation.6 | async-start | bytes 4718592 | tf_op jit(solution)/shard_map/all_to_all | solution.py:878
  311.1 91.9 %all-gather.3.cloned.1.call-start = ((), (), s32[]{:S(2)}) async-start(), calls=%async_computation.9 | async-start | bytes 2621440 | tf_op jit(solution)/shard_map/all_gather | solution.py:883
  317.2 48.9 %collective-permute-start.18 = (bf16[512,1024]{1,0:T(8,128)(2,1)}, bf16[512,1024]{1,0:T(8,128)(2,1)}, u32[]{:S(2)}, u32[]{:S(2)}) collective-permute-start(bf16[512,1024]{1,0:T(8,128)(2,1)} %get-tuple-element.94), channel_id=1, source_target_pairs={{0,8},{8,0},{16,24},{24,16},{1,9},{9,1},{17,25},{25,17},{2,10},{10... | collective-permute-start | bytes 3145736 | tf_op jit(solution)/shard_map/ppermute | solution.py:55
  322.9 57.7 %collective-permute-start.27 = (bf16[256,2048]{1,0:T(8,128)(2,1)}, bf16[256,2048]{1,0:T(8,128)(2,1)}, u32[]{:S(2)}, u32[]{:S(2)}) collective-permute-start(bf16[256,2048]{1,0:T(8,128)(2,1)} %in_other.1), channel_id=1, source_target_pairs={{0,8},{8,0},{16,24},{24,16},{1,9},{9,1},{17,25},{25,17},{2,10},{10... | collective-permute-start | bytes 3145736 | tf_op jit(solution)/shard_map/ppermute | solution.py:55
  365.4 10.2 %collective-permute-start.23 = (bf16[128,1152]{1,0:T(8,128)(2,1)}, bf16[128,1152]{1,0:T(8,128)(2,1)S(1)}, u32[]{:S(2)}, u32[]{:S(2)}) collective-permute-start(bf16[128,1152]{1,0:T(8,128)(2,1)} %reduce_sum.32.refs_0_), channel_id=1, source_target_pairs={{0,16},{8,24},{16,0},{24,8},{1,17},{9,25},{17,1},{25,9},{2,18},{10... | collective-permute-start | bytes 884744 | tf_op jit(solution)/shard_map/ppermute | solution.py:55
  367.3 23.2 %collective-permute-start.19 = (bf16[256,1024]{1,0:T(8,128)(2,1)S(1)}, bf16[256,1024]{1,0:T(8,128)(2,1)S(1)}, u32[]{:S(2)}, u32[]{:S(2)}) collective-permute-start(bf16[256,1024]{1,0:T(8,128)(2,1)S(1)} %add_convert_fusion.5), channel_id=1, source_target_pairs={{0,16},{8,24},{16,0},{24,8},{1,17},{9,25},{17,1},{25,9},{2,18},{10... | collective-permute-start | bytes 1572872 | tf_op jit(solution)/shard_map/ppermute | solution.py:55
  369.9 25.0 %collective-permute-start.24 = (bf16[128,1152]{1,0:T(8,128)(2,1)}, bf16[128,1152]{1,0:T(8,128)(2,1)S(1)}, u32[]{:S(2)}, u32[]{:S(2)}) collective-permute-start(bf16[128,1152]{1,0:T(8,128)(2,1)} %reduce_sum.32.refs_0_), channel_id=1, source_target_pairs={{0,8},{8,0},{16,24},{24,16},{1,9},{9,1},{17,25},{25,17},{2,10},{10... | collective-permute-start | bytes 884744 | tf_op jit(solution)/shard_map/ppermute | solution.py:55
  375.5 19.4 %collective-permute-start.25 = (bf16[128,1152]{1,0:T(8,128)(2,1)S(1)}, bf16[128,1152]{1,0:T(8,128)(2,1)S(1)}, u32[]{:S(2)}, u32[]{:S(2)}) collective-permute-start(bf16[128,1152]{1,0:T(8,128)(2,1)S(1)} %collective-permute-done.23.refs_1_), channel_id=1, source_target_pairs={{0,8},{8,0},{16,24},{24,16},{1,9},{9,1},{17,25},{25,17},{2,10},{10... | collective-permute-start | bytes 884744 | tf_op jit(solution)/shard_map/ppermute | solution.py:55
  (37 other events, 327.7 us)
Sparse Core Ops, SparseCore 0:
  262.9 44.6 reduce-scatter.1
  313.6 23.0 all-gather.2
